TPU v7x, 512 devices: a whole 4x4x16 slice. The times are simulated.
512 devices in a mesh: gx: 16 (over y, x_hi, core), gy: 32 (over x_lo, z).
Axes of the slice: x: 4 (x_hi: 2, x_lo: 2; x = x_hi * 2 + x_lo), y: 4, z: 16, core: 2. Of those that a mesh axis runs over, the one named last changes fastest.
Arguments:
- basis: bfloat16 [32, 256, 256, 128], P(None, 'gx', 'gy'), may hold values from -6 to 6
- phase_ids: int32 [256, 256, 128], P('gx', 'gy'), may hold values from 0 to 7
- phase_stiffness: bfloat16 [8], replicated, may hold values from 0.099609375 to 10
- owner_map: int32 [16, 32], P('gx'), may hold values from 0 to 31, as said below
Outputs:
- owned_diagonal: float32 [16, 96, 32, 32], P('gx', 'gy')
- owned_coupling: float32 [16, 96, 8, 32, 32], P('gx', 'gy')
Inputs may be any that keep to these rules, and one draw needn't show every extreme that they name: `owner_map`: in each grid row no owner holds more than 3 subdomains, and one owner holds exactly 3.
All inputs are finite; a program needn't handle non-finite values.
Results may differ from a plain program's by a relative error of at most 0.0003.
Values may be sent and summed in bfloat16 or wider, within the bound.
A program may use at most 64 MiB of HBM per device.

v0:
```python
import jax
import jax.numpy as jnp
from jax import lax
from jax.sharding import PartitionSpec as P

CAP = 3


REACT = 0.1
REGIONS = ((-1, -1), (-1, 0), (-1, 1), (0, -1), (0, 1), (1, -1), (1, 0), (1, 1))


def padded(block, sides, width):
    for axis, dim in sides:
        count = lax.axis_size(axis)
        forward = [(i, i + 1) for i in range(count - 1)]
        backward = [(target, source) for source, target in forward]
        low = lax.ppermute(
            lax.slice_in_dim(block, block.shape[dim] - width, None, axis=dim), axis, forward
        )
        high = lax.ppermute(lax.slice_in_dim(block, 0, width, axis=dim), axis, backward)
        block = jnp.concatenate([low, block, high], axis=dim)
    return block


def region_block(padb, padk, sx, sy):
    wx = padb.shape[1]
    wy = padb.shape[2]
    depth = padb.shape[3] - 2
    inner_x = wx - 2
    inner_y = wy - 2
    x_lo = inner_x - 1 if sx == 1 else 0
    x_hi = 1 if sx == -1 else inner_x
    y_lo = inner_y - 1 if sy == 1 else 0
    y_hi = 1 if sy == -1 else inner_y
    len_x = x_hi - x_lo
    len_y = y_hi - y_lo
    window = padb[:, x_lo : x_hi + 2, y_lo : y_hi + 2, :]
    kwin = padk[x_lo : x_hi + 2, y_lo : y_hi + 2, :]
    pos_x = jnp.arange(x_lo, x_hi + 2)
    pos_y = jnp.arange(y_lo, y_hi + 2)
    reg_x = jnp.where(pos_x == 0, -1, jnp.where(pos_x == wx - 1, 1, 0))
    reg_y = jnp.where(pos_y == 0, -1, jnp.where(pos_y == wy - 1, 1, 0))
    mask = ((reg_x == sx)[:, None] & (reg_y == sy)[None, :]).astype(window.dtype)
    zfield = window * mask[None, :, :, None]
    centre = window[:, 1 : 1 + len_x, 1 : 1 + len_y, 1 : 1 + depth].astype(jnp.float32)
    kcell = kwin[1 : 1 + len_x, 1 : 1 + len_y, 1 : 1 + depth]
    total = jnp.zeros(centre.shape, jnp.float32)
    diagsum = jnp.zeros(kcell.shape, jnp.float32)
    for ox in (-1, 0, 1):
        for oy in (-1, 0, 1):
            for oz in (-1, 0, 1):
                if ox == 0 and oy == 0 and (oz == 0):
                    continue
                coef = 1.0 / (9.0 * (ox * ox + oy * oy + oz * oz))
                kneigh = kwin[
                    1 + ox : 1 + ox + len_x, 1 + oy : 1 + oy + len_y, 1 + oz : 1 + oz + depth
                ]
                weight = coef * 2.0 * kcell * kneigh / (kcell + kneigh)
                near = zfield[
                    :, 1 + ox : 1 + ox + len_x, 1 + oy : 1 + oy + len_y, 1 + oz : 1 + oz + depth
                ]
                total = total - weight[None] * near.astype(jnp.float32)
                diagsum = diagsum + weight
    if sx == 0 and sy == 0:
        total = total + (diagsum + REACT * kcell)[None] * centre
    return jnp.einsum("kxyz,lxyz->kl", centre, total, precision=lax.Precision.HIGHEST)


def shards(basis, phase_ids, phase_stiffness, owner_map):
    stiffness = jnp.zeros(phase_ids.shape, jnp.bfloat16)
    for phase in range(phase_stiffness.shape[0]):
        stiffness = jnp.where(phase_ids == phase, phase_stiffness[phase], stiffness)
    window, wstiff = (
        padded(basis, (("gx", 1), ("gy", 2)), 1),
        padded(stiffness[None], (("gx", 1), ("gy", 2)), 1),
    )
    padb = jnp.pad(window, ((0, 0), (0, 0), (0, 0), (1, 1)))
    padk = jnp.pad(wstiff[0].astype(jnp.float32), ((0, 0), (0, 0), (1, 1)))
    cells = basis.shape[1] * basis.shape[2] * basis.shape[3]
    diagonal = region_block(padb, padk, 0, 0) / cells
    coupling = jnp.stack([region_block(padb, padk, sx, sy) for sx, sy in REGIONS])
    owners = owner_map[0]
    width = owners.shape[0]
    capacity = CAP
    column = jnp.arange(width, dtype=jnp.int32)
    mine = lax.axis_index("gy")
    own_owner = jnp.sum(jnp.where(column == mine, owners, 0))
    rank = jnp.sum(((column < mine) & (owners == own_owner)).astype(jnp.int32))
    slot = own_owner * capacity + rank
    onehot = (jnp.arange(width * capacity, dtype=jnp.int32) == slot).astype(jnp.float32)
    placed_diag = onehot[:, None, None] * diagonal[None]
    placed_coup = onehot[:, None, None, None] * coupling[None]
    owned_diag, owned_coup = (
        lax.psum_scatter(placed_diag, "gy", scatter_dimension=0, tiled=True),
        lax.psum_scatter(placed_coup, "gy", scatter_dimension=0, tiled=True),
    )
    return (owned_diag[None], owned_coup[None])


def solution(mesh):
    return jax.shard_map(
        shards,
        mesh=mesh,
        in_specs=(P(None, "gx", "gy", None), P("gx", "gy", None), P(), P("gx", None)),
        out_specs=(P("gx", "gy", None, None), P("gx", "gy", None, None, None)),
        check_vma=False,
    )
```

profile of v0, /device:TPU:24, one launch (start us, length us, event | category | flops | bytes accessed | tf_op | source)
XLA Modules:
  0.0 418.5 jit_solution(4590358832386918454)
XLA Ops:
  7.2 1.6 fusion.1348
  8.9 6.0 %fusion.690 = bf16[1,16,8,128]{3,2,1,0:T(8,128)(2,1)S(1)} fusion(s32[16,8,128]{2,1,0:T(8,128)} %param.5, bf16[]{:T(256)} %bitcast.8, bf16[]{:T(256)} %bitcast.7, bf16[]{:T(256)} %bitcast.6, bf16[]{:T(256)} %bitcast.5, bf16[]{:T(256)} %bitcast.4, bf16[]{:T(256)} %bitcast.3, bf16[]{:T(256)} %bitcast.2, bf16[]{:T(256)} %bitcast.1), kind=kLoop, calls=%fused_computation.905 | loop fusion | flops 262144 | bytes 98320 | tf_op jit(solution)/shard_map/broadcast_in_dim | solution.py:76
  14.9 1.9 collective-permute-start
  16.9 6.0 %collective-permute-start.1 = (bf16[1,1,8,128]{3,2,1,0:T(8,128)(2,1)S(1)}, bf16[1,1,8,128]{3,2,1,0:T(8,128)(2,1)S(1)}, u32[]{:S(2)}, u32[]{:S(2)}) collective-permute-start(bf16[1,1,8,128]{3,2,1,0:T(8,128)(2,1)S(1)} %get-tuple-element.256), channel_id=1, source_target_pairs={{32,0},{64,32},{96,64},{128,96},{160,128},{192,160},{224,192},{256... | collective-permute-start | bytes 6152 | tf_op jit(solution)/shard_map/ppermute | solution.py:21
  22.9 1.9 copy.51
  24.8 1.0 copy-done.1
  25.9 1.9 collective-permute-start.5
  27.8 2.4 collective-permute-start.4
  33.3 1.4 fusion.1226
  36.1 3.8 collective-permute-start.2
  39.9 1.3 collective-permute-start.3
  42.0 3.5 collective-permute-done.3
  45.5 0.7 fusion.1279
  46.2 0.7 fusion.1282
  48.2 0.7 fusion.1312
  48.9 0.7 fusion.1309
  52.8 0.7 divide_bitcast_fusion.38
  53.6 0.7 divide_bitcast_fusion.25
  54.3 0.7 divide_bitcast_fusion.51
  55.7 0.7 divide_bitcast_fusion.24
  56.4 0.7 add_divide_fusion.76
  57.1 0.7 add_divide_fusion.50
  57.8 0.9 add_divide_fusion.48
  58.7 0.9 add_divide_fusion.49
  59.5 0.9 add_divide_fusion.51
  60.4 0.8 add_divide_fusion.38
  61.2 1.5 multiply_add_fusion
  63.4 0.7 constant_dynamic-update-slice_fusion.1
  64.2 3.8 collective-permute-start.6
  68.1 1.5 collective-permute-start.7
  69.5 0.7 fusion.1229
  70.2 1.6 collective-permute-done.6
  71.8 5.5 %collective-permute-done.7 = bf16[32,18,1,128]{3,0,2,1:T(8,128)(2,1)S(1)} collective-permute-done((bf16[32,18,1,128]{3,0,2,1:T(8,128)(2,1)S(1)}, bf16[32,18,1,128]{3,0,2,1:T(8,128)(2,1)S(1)}, u32[]{:S(2)}, u32[]{:S(2)}) %collective-permute-start.7) | collective-permute-done | bytes 147488 | tf_op jit(solution)/shard_map/ppermute | solution.py:21
  77.3 3.8 broadcast_multiply_fusion.1
  81.1 26.6 %fusion.102 = f32[32,32]{0,1:T(8,128)} fusion(bf16[32,18,10,130]{3,0,2,1:T(8,128)(2,1)} %get-tuple-element.29, f32[16,8,128]{2,1,0:T(8,128)S(1)} %get-tuple-element.2, f32[16,8,128]{2,1,0:T(8,128)} %get-tuple-element.28, f32[16,8,128]{2,1,0:T(8,128)} %get-tuple-element.27, f32[16,8,128]{2,1,0:T(8,128)} %get-tuple-element.26, ...), kind=kOutput, calls=%fused_computation.272 | convolution fusion | flops 243794944 | bytes 31133696 | tf_op jit(solution)/shard_map/kxyz,lxyz->kl/dot_general | solution.py:67
  107.7 0.8 copy.56
  108.5 2.0 broadcast_multiply_fusion.2
  112.0 1.1 fusion.96
  113.3 1.6 fusion.95
  114.9 1.1 fusion.94
  116.4 2.2 fusion.98
  119.0 1.3 fusion.97
  120.6 1.1 fusion.93
  121.9 1.6 fusion.92
  123.8 1.0 fusion.91
  124.9 6.3 %broadcast_multiply_fusion = f32[96,8,32,32]{3,2,1,0:T(8,128)} fusion(f32[8,32,32]{2,1,0:T(8,128)S(1)} %copy.65, f32[96]{0:T(128)S(1)} %copy-done.83), kind=kLoop, calls=%fused_computation.164 | loop fusion | flops 786432 | bytes 3178880 | tf_op jit(solution)/shard_map/mul | solution.py:93
  131.2 118.3 %reduce-scatter.3.cloned.1.call-done = f32[3,32,32]{2,1,0:T(8,128)} async-done(((f32[96,32,32]{2,1,0:T(8,128)}), f32[3,32,32]{2,1,0:T(8,128)}) %reduce-scatter.3.cloned.1.call-update) | async-done | bytes 12304 | tf_op jit(solution)/shard_map/reduce_scatter | solution.py:95
  249.5 162.2 %reduce-scatter.5.cloned.1.call-done = f32[3,8,32,32]{3,2,1,0:T(8,128)} async-done(((f32[96,8,32,32]{3,2,1,0:T(8,128)}), f32[3,8,32,32]{3,2,1,0:T(8,128)}) %reduce-scatter.5.cloned.1.call-update) | async-done | bytes 98320 | tf_op jit(solution)/shard_map/reduce_scatter | solution.py:96
  (273 shorter events, 11.6 us)
Async XLA Ops:
  7.2 25.2 %copy-start = (bf16[32,16,8,128]{3,2,1,0:T(8,128)(2,1)S(1)}, bf16[32,16,8,128]{3,2,1,0:T(8,128)(2,1)}, u32[]{:S(2)}) copy-start(bf16[32,16,8,128]{3,2,1,0:T(8,128)(2,1)} %param.4) | copy-start | bytes 3145732
  7.2 25.5 %copy-start.115 = (s32[1,32]{1,0:T(1,128)S(1)}, s32[1,32]{1,0:T(1,128)}, u32[]{:S(2)}) copy-start(s32[1,32]{1,0:T(1,128)} %param.7) | copy-start | bytes 388
  7.2 242.3 %reduce-scatter.3.cloned.1.call-start = ((), (), s32[]{:S(2)}) async-start(), calls=%async_computation.2 | async-start | bytes 1622016 | tf_op jit(solution)/shard_map/reduce_scatter | solution.py:95
  14.9 21.1 %collective-permute-start = (bf16[1,1,8,128]{3,2,1,0:T(8,128)(2,1)S(1)}, bf16[1,1,8,128]{3,2,1,0:T(8,128)(2,1)S(1)}, u32[]{:S(2)}, u32[]{:S(2)}) collective-permute-start(bf16[1,1,8,128]{3,2,1,0:T(8,128)(2,1)S(1)} %get-tuple-element.255), channel_id=1, source_target_pairs={{0,32},{32,64},{64,96},{96,128},{128,160},{160,192},{192,224},{224... | collective-permute-start | bytes 6152 | tf_op jit(solution)/shard_map/ppermute | solution.py:18
  16.9 19.2 %collective-permute-start.1 = (bf16[1,1,8,128]{3,2,1,0:T(8,128)(2,1)S(1)}, bf16[1,1,8,128]{3,2,1,0:T(8,128)(2,1)S(1)}, u32[]{:S(2)}, u32[]{:S(2)}) collective-permute-start(bf16[1,1,8,128]{3,2,1,0:T(8,128)(2,1)S(1)} %get-tuple-element.256), channel_id=1, source_target_pairs={{32,0},{64,32},{96,64},{128,96},{160,128},{192,160},{224,192},{256... | collective-permute-start | bytes 6152 | tf_op jit(solution)/shard_map/ppermute | solution.py:21
  25.9 38.3 %collective-permute-start.5 = (bf16[32,1,8,128]{3,0,2,1:T(8,128)(2,1)S(1)}, bf16[32,1,8,128]{3,0,2,1:T(8,128)(2,1)S(1)}, u32[]{:S(2)}, u32[]{:S(2)}) collective-permute-start(bf16[32,1,8,128]{3,0,2,1:T(8,128)(2,1)S(1)} %get-tuple-element.43), channel_id=1, source_target_pairs={{32,0},{64,32},{96,64},{128,96},{160,128},{192,160},{224,192},{256... | collective-permute-start | bytes 196616 | tf_op jit(solution)/shard_map/ppermute | solution.py:21
  27.8 35.6 %collective-permute-start.4 = (bf16[32,1,8,128]{3,0,2,1:T(8,128)(2,1)S(1)}, bf16[32,1,8,128]{3,0,2,1:T(8,128)(2,1)S(1)}, u32[]{:S(2)}, u32[]{:S(2)}) collective-permute-start(bf16[32,1,8,128]{3,0,2,1:T(8,128)(2,1)S(1)} %get-tuple-element.44), channel_id=1, source_target_pairs={{0,32},{32,64},{64,96},{96,128},{128,160},{160,192},{192,224},{224... | collective-permute-start | bytes 196616 | tf_op jit(solution)/shard_map/ppermute | solution.py:18
  36.1 5.9 %collective-permute-start.2 = (bf16[1,18,1,128]{3,2,1,0:T(2,128)(2,1)S(1)}, bf16[1,18,1,128]{3,2,1,0:T(2,128)(2,1)S(1)}, u32[]{:S(2)}, u32[]{:S(2)}) collective-permute-start(bf16[1,18,1,128]{3,2,1,0:T(2,128)(2,1)S(1)} %get-tuple-element.253), channel_id=1, source_target_pairs={{0,1},{1,2},{2,3},{3,4},{4,5},{5,6},{6,7},{7,8},{8,9},{9,10},{10,1... | collective-permute-start | bytes 13832 | tf_op jit(solution)/shard_map/ppermute | solution.py:18
  39.9 5.6 %collective-permute-start.3 = (bf16[1,18,1,128]{3,2,1,0:T(2,128)(2,1)S(1)}, bf16[1,18,1,128]{3,2,1,0:T(2,128)(2,1)S(1)}, u32[]{:S(2)}, u32[]{:S(2)}) collective-permute-start(bf16[1,18,1,128]{3,2,1,0:T(2,128)(2,1)S(1)} %get-tuple-element.254), channel_id=1, source_target_pairs={{1,0},{2,1},{3,2},{4,3},{5,4},{6,5},{7,6},{8,7},{9,8},{10,9},{11,1... | collective-permute-start | bytes 13832 | tf_op jit(solution)/shard_map/ppermute | solution.py:21
  62.7 14.6 %copy-start.2 = (bf16[18,10]{1,0:T(8,128)(2,1)S(1)}, bf16[18,10]{1,0:T(8,128)(2,1)}, u32[]{:S(2)}) copy-start(bf16[18,10]{1,0:T(8,128)(2,1)} %and_convert_fusion) | copy-start | bytes 1084
  64.2 7.6 %collective-permute-start.6 = (bf16[32,18,1,128]{3,0,2,1:T(8,128)(2,1)S(1)}, bf16[32,18,1,128]{3,0,2,1:T(8,128)(2,1)S(1)}, u32[]{:S(2)}, u32[]{:S(2)}) collective-permute-start(bf16[32,18,1,128]{3,0,2,1:T(8,128)(2,1)S(1)} %get-tuple-element.39), channel_id=1, source_target_pairs={{0,1},{1,2},{2,3},{3,4},{4,5},{5,6},{6,7},{7,8},{8,9},{9,10},{10,1... | collective-permute-start | bytes 442376 | tf_op jit(solution)/shard_map/ppermute | solution.py:18
  68.1 9.3 %collective-permute-start.7 = (bf16[32,18,1,128]{3,0,2,1:T(8,128)(2,1)S(1)}, bf16[32,18,1,128]{3,0,2,1:T(8,128)(2,1)S(1)}, u32[]{:S(2)}, u32[]{:S(2)}) collective-permute-start(bf16[32,18,1,128]{3,0,2,1:T(8,128)(2,1)S(1)} %get-tuple-element.40), channel_id=1, source_target_pairs={{1,0},{2,1},{3,2},{4,3},{5,4},{6,5},{7,6},{8,7},{9,8},{10,9},{11,1... | collective-permute-start | bytes 442376 | tf_op jit(solution)/shard_map/ppermute | solution.py:21
  110.6 301.1 %reduce-scatter.5.cloned.1.call-start = ((), (), s32[]{:S(2)}) async-start(), calls=%async_computation.3 | async-start | bytes 12976128 | tf_op jit(solution)/shard_map/reduce_scatter | solution.py:96
  111.7 3.2 copy-start.109
  111.7 3.2 copy-start.110
  111.7 4.3 %copy-start.20 = (f32[16,1,128]{2,1,0:T(1,128)S(1)}, f32[16,1,128]{2,1,0:T(1,128)}, u32[]{:S(2)}) copy-start(f32[16,1,128]{2,1,0:T(1,128)} %get-tuple-element.170) | copy-start | bytes 24580
  111.7 4.3 %copy-start.21 = (f32[16,1,128]{2,1,0:T(1,128)S(1)}, f32[16,1,128]{2,1,0:T(1,128)}, u32[]{:S(2)}) copy-start(f32[16,1,128]{2,1,0:T(1,128)} %get-tuple-element.198) | copy-start | bytes 24580
  111.7 4.3 %copy-start.22 = (f32[16,1,128]{2,1,0:T(1,128)S(1)}, f32[16,1,128]{2,1,0:T(1,128)}, u32[]{:S(2)}) copy-start(f32[16,1,128]{2,1,0:T(1,128)} %get-tuple-element.199) | copy-start | bytes 24580
  111.7 4.3 %copy-start.23 = (f32[16,1,128]{2,1,0:T(1,128)S(1)}, f32[16,1,128]{2,1,0:T(1,128)}, u32[]{:S(2)}) copy-start(f32[16,1,128]{2,1,0:T(1,128)} %get-tuple-element.200) | copy-start | bytes 24580
  111.7 4.3 %copy-start.24 = (f32[16,1,128]{2,1,0:T(1,128)S(1)}, f32[16,1,128]{2,1,0:T(1,128)}, u32[]{:S(2)}) copy-start(f32[16,1,128]{2,1,0:T(1,128)} %get-tuple-element.201) | copy-start | bytes 24580
  111.7 4.3 %copy-start.25 = (f32[16,1,128]{2,1,0:T(1,128)S(1)}, f32[16,1,128]{2,1,0:T(1,128)}, u32[]{:S(2)}) copy-start(f32[16,1,128]{2,1,0:T(1,128)} %get-tuple-element.202) | copy-start | bytes 24580
  111.8 4.3 %copy-start.26 = (f32[16,1,128]{2,1,0:T(1,128)S(1)}, f32[16,1,128]{2,1,0:T(1,128)}, u32[]{:S(2)}) copy-start(f32[16,1,128]{2,1,0:T(1,128)} %get-tuple-element.203) | copy-start | bytes 24580
  111.8 4.3 %copy-start.27 = (f32[16,1,128]{2,1,0:T(1,128)S(1)}, f32[16,1,128]{2,1,0:T(1,128)}, u32[]{:S(2)}) copy-start(f32[16,1,128]{2,1,0:T(1,128)} %get-tuple-element.204) | copy-start | bytes 24580
  111.8 4.3 %copy-start.37 = (f32[16,1,128]{2,1,0:T(1,128)S(1)}, f32[16,1,128]{2,1,0:T(1,128)}, u32[]{:S(2)}) copy-start(f32[16,1,128]{2,1,0:T(1,128)} %get-tuple-element.181) | copy-start | bytes 24580
  111.8 4.3 %copy-start.38 = (f32[16,1,128]{2,1,0:T(1,128)S(1)}, f32[16,1,128]{2,1,0:T(1,128)}, u32[]{:S(2)}) copy-start(f32[16,1,128]{2,1,0:T(1,128)} %get-tuple-element.182) | copy-start | bytes 24580
  111.8 4.3 %copy-start.39 = (f32[16,1,128]{2,1,0:T(1,128)S(1)}, f32[16,1,128]{2,1,0:T(1,128)}, u32[]{:S(2)}) copy-start(f32[16,1,128]{2,1,0:T(1,128)} %get-tuple-element.172) | copy-start | bytes 24580
  111.8 4.3 %copy-start.40 = (f32[16,1,128]{2,1,0:T(1,128)S(1)}, f32[16,1,128]{2,1,0:T(1,128)}, u32[]{:S(2)}) copy-start(f32[16,1,128]{2,1,0:T(1,128)} %get-tuple-element.173) | copy-start | bytes 24580
  111.8 4.3 %copy-start.41 = (f32[16,1,128]{2,1,0:T(1,128)S(1)}, f32[16,1,128]{2,1,0:T(1,128)}, u32[]{:S(2)}) copy-start(f32[16,1,128]{2,1,0:T(1,128)} %get-tuple-element.174) | copy-start | bytes 24580
  111.8 4.3 %copy-start.42 = (f32[16,1,128]{2,1,0:T(1,128)S(1)}, f32[16,1,128]{2,1,0:T(1,128)}, u32[]{:S(2)}) copy-start(f32[16,1,128]{2,1,0:T(1,128)} %get-tuple-element.175) | copy-start | bytes 24580
  120.3 3.2 copy-start.84
  120.4 3.1 copy-start.85
  120.4 3.1 copy-start.86
  120.4 3.1 copy-start.87
  120.4 3.1 copy-start.88
  120.4 3.1 copy-start.89
  120.4 3.1 copy-start.90
  120.4 3.1 copy-start.91
  120.5 3.1 copy-start.92
  120.5 3.1 copy-start.93
  120.5 3.1 copy-start.94
  120.5 3.1 copy-start.95
  120.5 3.1 copy-start.96
  120.5 3.1 copy-start.97
  120.5 3.1 copy-start.98
  120.5 3.1 copy-start.99
  120.5 3.1 copy-start.100
  120.5 3.1 copy-start.101
  120.6 4.2 %copy-start.83 = (f32[96]{0:T(128)S(1)}, f32[96]{0:T(128)}, u32[]{:S(2)}) copy-start(f32[96]{0:T(128)} %compare_convert_fusion) | copy-start | bytes 1156
  (78 other events, 188.4 us)
Sparse Core Ops, SparseCore 0:
  110.7 138.7 reduce-scatter.2
  253.1 158.4 reduce-scatter.4
where the time goes:
time: 420 us; the launch traced here: 418 us
  waiting for transfers between devices  291 us (69%)
  other arithmetic  42 us (10%)
  matrix products  37.5 us (9%)
  starting transfers between devices  23 us (5%)
  between operations  17.4 us (4%)
  local copies, waits for them, and re-layouts  7.6 us (2%)
    reduce_scatter x1, waiting for transfers between devices, shards(): lax.psum_scatter(placed_coup, 'gy', scatter_dimension=0, tiled=True)  162 us
    reduce_scatter x1, waiting for transfers between devices, shards(): lax.psum_scatter(placed_diag, 'gy', scatter_dimension=0, tiled=True)  118 us
    dot_general x9, matrix products, region_block(): jnp.einsum('kxyz,lxyz->kl', centre, total, precision=lax.Precision.HIGHEST)  37.5 us
    mul x18, other arithmetic, region_block(): total = total - weight[None] * near.astype(jnp.float32)  12.2 us
    ppermute x4, starting transfers between devices, padded(): lax.ppermute(lax.slice_in_dim(block, block.shape[dim] - width, None, axis...  12 us
    ppermute x4, starting transfers between devices, padded(): lax.ppermute(lax.slice_in_dim(block, 0, width, axis=dim), axis, backward)  10.7 us
    ppermute x4, waiting for transfers between devices, padded(): lax.ppermute(lax.slice_in_dim(block, 0, width, axis=dim), axis, backward)  8.97 us
  transfers between devices with their start and end apart: 10, of which 5 were waited for; matrix products, arithmetic and copies ran while one was open for 11% of the time, Pallas kernels for 0%

commit v1 on v0

v1 whole, which is shorter than its diff:
```python
import functools

import jax
import jax.numpy as jnp
from jax import lax
from jax.experimental import pallas as pl
from jax.experimental.pallas import tpu as pltpu
from jax.sharding import PartitionSpec as P

CAP = 3
REACT = 0.1
REGIONS = ((-1, -1), (-1, 0), (-1, 1), (0, -1), (0, 1), (1, -1), (1, 0), (1, 1))
CORNERS = ((-1, -1), (-1, 1), (1, -1), (1, 1))
OFFSETS = [
    (ox, oy, oz)
    for ox in (-1, 0, 1)
    for oy in (-1, 0, 1)
    for oz in (-1, 0, 1)
    if (ox, oy, oz) != (0, 0, 0)
]
INDEX = {o: i for i, o in enumerate(OFFSETS)}
HALF = [o for o in OFFSETS if o[2] == 1] + [(0, 1, 0), (1, -1, 0), (1, 0, 0), (1, 1, 0)]
MESH = pl.DeviceIdType.MESH
K, CX, CY, NZ = 32, 16, 8, 128
ROWS, COLS = 16, 32
LAST = (((1,), (1,)), ((), ()))


def split(value):
    high = value.astype(jnp.bfloat16)
    low = (value - high.astype(jnp.float32)).astype(jnp.bfloat16)
    return high, low


def kernel(
    basis,
    ids,
    phase,
    owner,
    out_diag,
    out_coup,
    raw,
    stage,
    zf,
    zs,
    zb,
    kp,
    kz,
    kface,
    kx,
    ky,
    hx,
    hy,
    hc,
    fx,
    fy,
    fc,
    weights,
    dsum,
    yb,
    piece,
    pieces,
    slots,
    owned,
    load_sem,
    ks_send,
    ks_recv,
    z_send,
    z_recv,
    one_send,
    one_recv,
    two_send,
    two_recv,
    local_sem,
):
    f32 = jnp.float32
    ax = lax.axis_index("gx")
    ay = lax.axis_index("gy")

    def device(dx, dy):
        return (lax.rem(ax + dx + ROWS, ROWS), lax.rem(ay + dy + COLS, COLS))

    loads = [
        pltpu.make_async_copy(
            basis.at[pl.ds(1024 * g, 1024)], raw.at[pl.ds(1024 * g, 1024)], load_sem.at[g]
        )
        for g in range(4)
    ]
    for copy in loads:
        copy.start()

    barrier = pltpu.get_barrier_semaphore()

    def greet(off, carry):
        pl.semaphore_signal(
            barrier, inc=1, device_id=(ax, lax.rem(ay + off, COLS)), device_id_type=MESH
        )
        return carry

    for dx, dy in REGIONS:
        if dx != 0:
            pl.semaphore_signal(barrier, inc=1, device_id=device(dx, dy), device_id_type=MESH)
    lax.fori_loop(1, COLS, greet, 0)

    table = phase[...].astype(f32)
    kp[...] = jnp.zeros_like(kp)
    for x in range(CX):
        cell = ids[x]
        value = jnp.zeros((CY, NZ), f32)
        for p in range(8):
            value = jnp.where(cell == p, table[0:1, p : p + 1], value)
        kp[x + 1, 8:16, :] = value
    for side, y in ((0, 0), (1, CY - 1)):
        for x in range(CX):
            kface[side, x : x + 1, :] = kp[x + 1, 8 + y : 9 + y, :]

    pl.semaphore_wait(barrier, COLS - 1 + 6)

    sends = []
    for i, (dx, dy) in enumerate(REGIONS):
        other = REGIONS.index((-dx, -dy))
        if dx == 0:
            src, dst = kface.at[0 if dy < 0 else 1], ky.at[0 if dy > 0 else 1]
        else:
            src, dst = kp.at[1 if dx < 0 else CX, pl.ds(8, 8), :], kx.at[other]
        sends.append(
            pltpu.make_async_remote_copy(
                src_ref=src,
                dst_ref=dst,
                send_sem=ks_send.at[i],
                recv_sem=ks_recv.at[other],
                device_id=device(dx, dy),
                device_id_type=MESH,
            )
        )
    for copy in sends:
        copy.start()

    for g in range(4):
        loads[g].wait()

        def widen(i, carry, g=g):
            at = pl.multiple_of(1024 * g + i * 128, 128)
            stage[pl.ds(at, 128), :] = raw[pl.ds(at, 128), :].astype(f32)
            return carry

        lax.fori_loop(0, 8, widen, 0)
    zero = jnp.zeros((8, K, NZ), f32)
    for edge in (0, CX + 1):
        zf[edge] = zero
        zs[edge] = zero

    def turn(x, carry):
        for y in range(CY):
            r = x * CY + y
            slab = jnp.concatenate(
                [stage[pl.ds(1024 * g + r, 8, stride=128), :] for g in range(4)], axis=0
            )
            zf[x + 1, y] = slab
            zs[x + 1, y] = pltpu.roll(slab, NZ - 1, 1)
            zb[x, y] = slab.astype(jnp.bfloat16)
        return carry

    lax.fori_loop(0, CX, turn, 0)

    moves = []
    for i, (dx, dy) in enumerate(REGIONS):
        other = REGIONS.index((-dx, -dy))
        x_at = 0 if dx < 0 else CX - 1
        y_at = 0 if dy < 0 else CY - 1
        if dx == 0:
            src, dst = zb.at[:, y_at], hy.at[0 if dy > 0 else 1]
        elif dy == 0:
            src, dst = zb.at[x_at], hx.at[0 if dx > 0 else 1]
        else:
            src, dst = zb.at[x_at, y_at], hc.at[CORNERS.index((-dx, -dy))]
        moves.append(
            pltpu.make_async_remote_copy(
                src_ref=src,
                dst_ref=dst,
                send_sem=z_send.at[i],
                recv_sem=z_recv.at[other],
                device_id=device(dx, dy),
                device_id_type=MESH,
            )
        )
    for i in (3, 4, 1, 6, 0, 2, 5, 7):
        moves[i].start()

    for copy in sends:
        copy.wait()
    low_x = (ax > 0).astype(f32)
    high_x = (ax < ROWS - 1).astype(f32)
    low_y = (ay > 0).astype(f32)
    high_y = (ay < COLS - 1).astype(f32)
    for dx, at, keep in ((-1, 0, low_x), (1, CX + 1, high_x)):
        kp[at, 8:16, :] = kx[REGIONS.index((dx, 0))] * keep
        kp[at, 7:8, :] = kx[REGIONS.index((dx, -1)), 7:8, :] * (keep * low_y)
        kp[at, 16:17, :] = kx[REGIONS.index((dx, 1)), 0:1, :] * (keep * high_y)
    for x in range(CX):
        kp[x + 1, 7:8, :] = ky[0, x : x + 1, :] * low_y
        kp[x + 1, 16:17, :] = ky[1, x : x + 1, :] * high_y
    lane = lax.broadcasted_iota(jnp.int32, (24, NZ), 1)
    for x in range(CX + 2):
        row = kp[x]
        kz[0, x] = jnp.where(lane == 0, 0.0, pltpu.roll(row, 1, 1))
        kz[1, x] = jnp.where(lane == NZ - 1, 0.0, pltpu.roll(row, NZ - 1, 1))

    def weigh(x, carry):
        own = kp[x + 1, 8:16, :]
        total = REACT * own
        for ox, oy, oz in OFFSETS:
            frame = kp if oz == 0 else kz.at[0 if oz < 0 else 1]
            near = frame[x + 1 + ox, 8 + oy : 16 + oy, :]
            coef = 2.0 / (9.0 * (ox * ox + oy * oy + oz * oz))
            weight = (coef * own) * near / (own + near)
            weights[INDEX[(ox, oy, oz)], x] = weight
            total = total + weight
        dsum[x] = 0.5 * total
        return carry

    lax.fori_loop(0, CX, weigh, 0)

    def interior(x, acc):
        for y in range(CY):
            value = dsum[x, y : y + 1, :] * zf[x + 1, y]
            for ox, oy, oz in HALF:
                if not 0 <= y + oy < CY:
                    continue
                field = zf if oz == 0 else zs
                w = weights[INDEX[(ox, oy, oz)], x, y : y + 1, :]
                value = value - w * field[x + 1 + ox, y + oy]
            high, low = split(value)
            yb[y, 0:K, :] = high
            yb[y, K : 2 * K, :] = low
        left = jnp.concatenate([zb[x, y] for y in range(CY)], axis=1)
        right = jnp.concatenate([yb[y] for y in range(CY)], axis=1)
        return acc + lax.dot_general(left, right, LAST, preferred_element_type=f32)

    acc = lax.fori_loop(0, CX, interior, jnp.zeros((K, 2 * K), f32))
    half = acc[:, :K] + acc[:, K:]
    diagonal = (half + half.T) * (1.0 / (CX * CY * NZ))

    for copy in moves:
        copy.wait()

    def spread(slab, dst, index):
        value = slab.astype(f32)
        dst[(1,) + index] = value
        dst[(0,) + index] = pltpu.roll(value, 1, 1)
        dst[(2,) + index] = pltpu.roll(value, NZ - 1, 1)

    edge = jnp.zeros((K, NZ), f32)
    for side in range(2):
        for y in range(CY):
            spread(hx[side, y], fx, (side, y))

        def spread_y(x, carry, side=side):
            spread(hy[side, x], fy, (side, x + 1))
            return carry

        lax.fori_loop(0, CX, spread_y, 0)
        for o in range(3):
            fy[o, side, 0] = edge
            fy[o, side, CX + 1] = edge
    for c in range(4):
        spread(hc[c], fc, (c,))

    blocks = {}

    def image(region, x, y, fetch):
        value = jnp.zeros((K, NZ), f32)
        for offset, field in fetch:
            value = value - weights[INDEX[offset], x, y : y + 1, :] * field
        return split(value)

    def finish(product):
        return product[:, :K] + product[:, K:]

    for side, dx in ((0, -1), (1, 1)):
        x = 0 if dx < 0 else CX - 1
        for y in range(CY):
            high, low = image(
                (dx, 0),
                x,
                y,
                [
                    ((dx, oy, oz), fx[oz + 1, side, y + oy])
                    for oy in (-1, 0, 1)
                    if 0 <= y + oy < CY
                    for oz in (-1, 0, 1)
                ],
            )
            yb[y, 0:K, :] = high
            yb[y, K : 2 * K, :] = low
        left = jnp.concatenate([zb[x, y] for y in range(CY)], axis=1)
        right = jnp.concatenate([yb[y] for y in range(CY)], axis=1)
        blocks[(dx, 0)] = finish(
            lax.dot_general(left, right, LAST, preferred_element_type=f32)
        )
    for side, dy in ((0, -1), (1, 1)):
        y = 0 if dy < 0 else CY - 1

        def face(x, carry, side=side, dy=dy, y=y):
            high, low = image(
                (0, dy),
                x,
                y,
                [
                    ((ox, dy, oz), fy[oz + 1, side, x + 1 + ox])
                    for ox in (-1, 0, 1)
                    for oz in (-1, 0, 1)
                ],
            )
            yb[x, 0:K, :] = high
            yb[x, K : 2 * K, :] = low
            return carry

        lax.fori_loop(0, CX, face, 0)
        left = jnp.concatenate([zb[x, y] for x in range(CX)], axis=1)
        right = jnp.concatenate([yb[x] for x in range(CX)], axis=1)
        blocks[(0, dy)] = finish(
            lax.dot_general(left, right, LAST, preferred_element_type=f32)
        )
    for c, (dx, dy) in enumerate(CORNERS):
        x = 0 if dx < 0 else CX - 1
        y = 0 if dy < 0 else CY - 1
        high, low = image(
            (dx, dy), x, y, [((dx, dy, oz), fc[oz + 1, c]) for oz in (-1, 0, 1)]
        )
        right = jnp.concatenate([high, low], axis=0)
        blocks[(dx, dy)] = finish(
            lax.dot_general(zb[x, y], right, LAST, preferred_element_type=f32)
        )

    width = COLS
    own_row = jnp.broadcast_to(owner[...], (width, width))
    i_sub = lax.broadcasted_iota(jnp.int32, (width, width), 0)
    i_lane = lax.broadcasted_iota(jnp.int32, (width, width), 1)
    own_f = own_row.astype(f32)
    own_col = jnp.sum(jnp.where(i_sub == i_lane, own_f, 0.0), axis=1, keepdims=True)
    before = (own_col == own_f) & (i_sub < i_lane)
    rank = jnp.sum(jnp.where(before, 1.0, 0.0), axis=0, keepdims=True)
    code = jnp.broadcast_to(own_f[0:1] * 4.0 + rank, (8, width)).astype(jnp.bfloat16)
    e_sub = lax.broadcasted_iota(jnp.int32, (width, NZ), 0)
    e_lane = lax.broadcasted_iota(jnp.int32, (width, NZ), 1)
    expand = jnp.where(e_lane // 4 == e_sub, 1.0, 0.0).astype(jnp.bfloat16)
    wide = jnp.dot(code, expand, preferred_element_type=f32)[0:1].astype(jnp.int32)
    wide_owner = wide // 4
    wide_rank = wide - wide_owner * 4
    lane1 = lax.broadcasted_iota(jnp.int32, (1, NZ), 1)
    part = lane1 - (lane1 // 4) * 4
    target = wide_owner * 8 + jnp.where(part < 2, wide_rank * 2 + part, 6)
    target = jnp.where(part < 3, target, -1)
    p_sub = lax.broadcasted_iota(jnp.int32, (COLS * 8, NZ), 0)
    route = jnp.where(p_sub == target, 1.0, 0.0).astype(jnp.bfloat16)
    my_rank = jnp.sum(
        jnp.where(lax.broadcasted_iota(jnp.int32, (1, width), 1) == ay, rank, 0.0),
        axis=1,
        keepdims=True,
    )
    quarter = (lax.broadcasted_iota(jnp.int32, (K, NZ), 1) // K).astype(f32)

    order = [blocks[t] for t in REGIONS]
    rows = [
        jnp.concatenate(order[:4], axis=1),
        jnp.concatenate(order[4:], axis=1),
        jnp.where(quarter == my_rank, jnp.concatenate([diagonal] * 4, axis=1), 0.0),
    ]
    flat = piece.reshape(4 * K, NZ)
    for l, value in enumerate(rows + [jnp.zeros((K, NZ), f32)]):
        flat[pl.ds(l, K, stride=4), :] = value

    def first(off, carry):
        to = lax.rem(ay + off, COLS)
        pltpu.make_async_remote_copy(
            src_ref=piece.at[to],
            dst_ref=pieces.at[ay],
            send_sem=one_send,
            recv_sem=one_recv,
            device_id=(ax, to),
            device_id_type=MESH,
        ).start()
        return carry

    lax.fori_loop(1, COLS, first, 0)
    keep = pltpu.make_async_copy(piece.at[ay], pieces.at[ay], local_sem.at[0])
    keep.start()
    keep.wait()
    many = pieces.at[pl.ds(0, COLS - 1)]
    pltpu.make_async_copy(many, many, one_recv).wait()

    got = pieces.reshape(4 * COLS, NZ)[...]
    a1 = got.astype(jnp.bfloat16)
    rest = got - a1.astype(f32)
    a2 = rest.astype(jnp.bfloat16)
    a3 = (rest - a2.astype(f32)).astype(jnp.bfloat16)
    slots[...] = (
        jnp.dot(route, a1, preferred_element_type=f32)
        + jnp.dot(route, a2, preferred_element_type=f32)
        + jnp.dot(route, a3, preferred_element_type=f32)
    ).reshape(COLS, 8, NZ)

    def second(off, carry):
        to = lax.rem(ay + off, COLS)
        pltpu.make_async_remote_copy(
            src_ref=slots.at[to],
            dst_ref=owned.at[ay],
            send_sem=two_send,
            recv_sem=two_recv,
            device_id=(ax, to),
            device_id_type=MESH,
        ).start()
        return carry

    lax.fori_loop(1, COLS, second, 0)
    keep = pltpu.make_async_copy(slots.at[ay], owned.at[ay], local_sem.at[1])
    keep.start()
    keep.wait()
    sent = piece.at[pl.ds(0, COLS - 1)]
    pltpu.make_async_copy(sent, sent, one_send).wait()
    many = owned.at[pl.ds(0, COLS - 1)]
    pltpu.make_async_copy(many, many, two_recv).wait()

    mine = owned.reshape(8 * COLS, NZ)
    for c in range(CAP):
        for half_row in range(2):
            value = mine[pl.ds(2 * c + half_row, K, stride=8), :]
            for q in range(4):
                out_coup[c, half_row * 4 + q] = value[:, q * K : (q + 1) * K]
    value = mine[pl.ds(6, K, stride=8), :]
    for c in range(CAP):
        out_diag[c] = value[:, c * K : (c + 1) * K]
    sent = slots.at[pl.ds(0, COLS - 1)]
    pltpu.make_async_copy(sent, sent, two_send).wait()


def shards(basis, phase_ids, phase_stiffness, owner_map):
    f32, bf16 = jnp.float32, jnp.bfloat16
    vmem = pltpu.VMEM
    dma = pltpu.SemaphoreType.DMA
    whole = pl.BlockSpec(memory_space=pltpu.VMEM)
    diag, coup = pl.pallas_call(
        kernel,
        out_shape=(
            jax.ShapeDtypeStruct((CAP, K, K), f32),
            jax.ShapeDtypeStruct((CAP, 8, K, K), f32),
        ),
        in_specs=[pl.BlockSpec(memory_space=pl.ANY), whole, whole, whole],
        out_specs=(whole, whole),
        scratch_shapes=[
            vmem((K * CX * CY, NZ), bf16),
            vmem((K * CX * CY, NZ), f32),
            vmem((CX + 2, CY, K, NZ), f32),
            vmem((CX + 2, CY, K, NZ), f32),
            vmem((CX, CY, K, NZ), bf16),
            vmem((CX + 2, 24, NZ), f32),
            vmem((2, CX + 2, 24, NZ), f32),
            vmem((2, CX, NZ), f32),
            vmem((8, 8, NZ), f32),
            vmem((2, CX, NZ), f32),
            vmem((2, CY, K, NZ), bf16),
            vmem((2, CX, K, NZ), bf16),
            vmem((4, K, NZ), bf16),
            vmem((3, 2, CY, K, NZ), f32),
            vmem((3, 2, CX + 2, K, NZ), f32),
            vmem((3, 4, K, NZ), f32),
            vmem((26, CX, CY, NZ), f32),
            vmem((CX, CY, NZ), f32),
            vmem((CX, 2 * K, NZ), bf16),
            vmem((K, 4, NZ), f32),
            vmem((COLS, 4, NZ), f32),
            vmem((COLS, 8, NZ), f32),
            vmem((COLS, 8, NZ), f32),
            dma((4,)),
            dma((8,)),
            dma((8,)),
            dma((8,)),
            dma((8,)),
            dma,
            dma,
            dma,
            dma,
            dma((2,)),
        ],
        compiler_params=pltpu.CompilerParams(
            collective_id=0, has_side_effects=True, vmem_limit_bytes=48 * 1024 * 1024
        ),
    )(
        basis.reshape(K * CX * CY, NZ),
        phase_ids,
        phase_stiffness.reshape(1, 8),
        owner_map,
    )
    return diag[None], coup[None]


def solution(mesh):
    return jax.shard_map(
        shards,
        mesh=mesh,
        in_specs=(P(None, "gx", "gy", None), P("gx", "gy", None), P(), P("gx", None)),
        out_specs=(P("gx", "gy", None, None), P("gx", "gy", None, None, None)),
        check_vma=False,
    )
```

time: 420 us -> 54.5 us (0.13)
  waiting for transfers between devices: 291 us -> 0 us
  Pallas kernels: 0 us -> 48.7 us
  other arithmetic: 42 us -> 0 us
  matrix products: 37.5 us -> 0 us
  starting transfers between devices: 23 us -> 0 us
  between operations: 17.4 us -> 0.66 us
    reduce_scatter x2 -> x0, waiting for transfers between devices: 280 us -> none  [the longest x1 162 us: shards(): lax.psum_scatter(placed_coup, 'gy', scatter_dimension=0, tiled=True)]
    pallas_call x0 -> x1, Pallas kernels: none -> 48.7 us  [shards(): pl.pallas_call(kernel, out_shape=(jax.ShapeDtypeStruct((CAP, K, K), f32),...]
    dot_general x9 -> x0, matrix products: 37.5 us -> none  [region_block(): jnp.einsum('kxyz,lxyz->kl', centre, total, precision=lax.Precision.HIGHEST)]
    mul x24 -> x0, other arithmetic: 24.8 us -> none  [the longest x18 12.2 us: region_block(): total = total - weight[None] * near.astype(jnp.float32)]
    ppermute x8 -> x0, starting transfers between devices: 22.7 us -> none  [the longest x4 12 us: padded(): lax.ppermute(lax.slice_in_dim(block, block.shape[dim] - width, None, axis...]
    ppermute x8 -> x0, waiting for transfers between devices: 10.5 us -> none  [the longest x4 8.97 us: padded(): lax.ppermute(lax.slice_in_dim(block, 0, width, axis=dim), axis, backward)]
    broadcast_in_dim x1 -> x0, other arithmetic: 6.05 us -> none  [shards(): stiffness[None]]
    div x6 -> x0, other arithmetic: 4.86 us -> none  [region_block(): weight = coef * 2.0 * kcell * kneigh / (kcell + kneigh)]
  transfers between devices with their start and end apart: 10 -> 0, of which waited for: 5 -> 0; matrix products, arithmetic and copies ran while one was open for 11% -> 0% of each run, Pallas kernels for 0% -> 0%
where the time goes in v1:
time: 54.5 us; the launch traced here: 53.5 us
  Pallas kernels  48.7 us (89%)
  local copies, waits for them, and re-layouts  4.09 us (8%)
  between operations  0.66 us (1%)
    pallas_call x1, Pallas kernels, shards(): pl.pallas_call(kernel, out_shape=(jax.ShapeDtypeStruct((CAP, K, K), f32),...  48.7 us
    unnamed x10, local copies, waits for them, and re-layouts  4.09 us

profile of v1, /device:TPU:24, one launch (start us, length us, event | category | flops | bytes accessed | tf_op | source)
XLA Modules:
  0.0 53.5 jit_solution(10701105747665313778)
XLA Ops:
  0.6 0.0 copy-start.2
  0.6 0.0 copy-start.3
  0.7 0.6 %copy-done.2 = bf16[8]{0:T(256)(128)(2,1)S(1)} copy-done((bf16[8]{0:T(256)(128)(2,1)S(1)}, bf16[8]{0:T(256)(128)(2,1)}, u32[]{:S(2)}) %copy-start.2) | copy-done | bytes 40
  1.3 0.0 copy-done.3
  1.3 0.0 copy-start
  1.3 1.2 %copy-done = bf16[32,16,8,128]{3,2,1,0:T(8,128)(2,1)S(1)} copy-done((bf16[32,16,8,128]{3,2,1,0:T(8,128)(2,1)S(1)}, bf16[32,16,8,128]{3,2,1,0:T(8,128)(2,1)}, u32[]{:S(2)}) %copy-start) | copy-done | bytes 1048600
  2.5 0.0 copy-start.1
  2.5 0.8 %copy-done.1 = s32[16,8,128]{2,1,0:T(8,128)S(1)} copy-done((s32[16,8,128]{2,1,0:T(8,128)S(1)}, s32[16,8,128]{2,1,0:T(8,128)}, u32[]{:S(2)}) %copy-start.1) | copy-done | bytes 65560
  3.4 48.7 %shard_map.59 = (f32[3,32,32]{2,1,0:T(8,128)S(1)}, f32[3,8,32,32]{3,2,1,0:T(8,128)S(1)}) custom-call(bf16[4096,128]{1,0:T(8,128)(2,1)S(1)} %bitcast.4, s32[16,8,128]{2,1,0:T(8,128)S(1)} %copy-done.1, bf16[1,8]{1,0:T(2,128)(2,1)S(1)} %bitcast.7, s32[1,32]{1,0:T(1,128)S(1)} %copy-done.3), custom_call_target="tpu_custom_call" | custom-call | tf_op jit(solution)/shard_map/pallas_call | solution.py:443
  52.1 0.6 %copy.8 = f32[1,3,32,32]{3,2,1,0:T(8,128)} copy(f32[1,3,32,32]{3,2,1,0:T(8,128)S(1)} %bitcast.6) | data formatting | bytes 24576
  52.7 0.7 %copy.9 = f32[1,3,8,32,32]{4,3,2,1,0:T(8,128)} copy(f32[1,3,8,32,32]{4,3,2,1,0:T(8,128)S(1)} %bitcast.5) | data formatting | bytes 196608
Async XLA Ops:
  0.6 0.7 %copy-start.2 = (bf16[8]{0:T(256)(128)(2,1)S(1)}, bf16[8]{0:T(256)(128)(2,1)}, u32[]{:S(2)}) copy-start(bf16[8]{0:T(256)(128)(2,1)} %param.6) | copy-start | bytes 52
  0.6 0.7 %copy-start.3 = (s32[1,32]{1,0:T(1,128)S(1)}, s32[1,32]{1,0:T(1,128)}, u32[]{:S(2)}) copy-start(s32[1,32]{1,0:T(1,128)} %owner.1) | copy-start | bytes 388
  1.3 1.2 %copy-start = (bf16[32,16,8,128]{3,2,1,0:T(8,128)(2,1)S(1)}, bf16[32,16,8,128]{3,2,1,0:T(8,128)(2,1)}, u32[]{:S(2)}) copy-start(bf16[32,16,8,128]{3,2,1,0:T(8,128)(2,1)} %param.4) | copy-start | bytes 3145732
  2.5 0.8 %copy-start.1 = (s32[16,8,128]{2,1,0:T(8,128)S(1)}, s32[16,8,128]{2,1,0:T(8,128)}, u32[]{:S(2)}) copy-start(s32[16,8,128]{2,1,0:T(8,128)} %ids.1) | copy-start | bytes 196612

commit v2 on v1

v2 whole, which is shorter than its diff:
```python
import functools

import jax
import jax.numpy as jnp
from jax import lax
from jax.experimental import pallas as pl
from jax.experimental.pallas import tpu as pltpu
from jax.sharding import PartitionSpec as P

CAP = 3
REACT = 0.1
REGIONS = ((-1, -1), (-1, 0), (-1, 1), (0, -1), (0, 1), (1, -1), (1, 0), (1, 1))
CORNERS = ((-1, -1), (-1, 1), (1, -1), (1, 1))
OFFSETS = [
    (ox, oy, oz)
    for ox in (-1, 0, 1)
    for oy in (-1, 0, 1)
    for oz in (-1, 0, 1)
    if (ox, oy, oz) != (0, 0, 0)
]
HALF = [o for o in OFFSETS if o[2] == 1] + [(0, 1, 0), (1, -1, 0), (1, 0, 0), (1, 1, 0)]
MESH = pl.DeviceIdType.MESH
K, CX, CY, NZ = 32, 16, 8, 128
ROWS, COLS = 16, 32
PITCH = 136
LAST = (((1,), (1,)), ((), ()))


def split(value):
    high = value.astype(jnp.bfloat16)
    low = (value - high.astype(jnp.float32)).astype(jnp.bfloat16)
    return high, low


def kernel(
    basis,
    ids_hbm,
    phase_hbm,
    owner_hbm,
    out_diag,
    out_coup,
    raw,
    ids,
    phase,
    owner,
    stage,
    zf,
    zs,
    zb,
    zmx,
    zmy,
    kp,
    kz,
    kx,
    ky,
    kface,
    frame_x,
    frame_y,
    frame_own,
    hx,
    hy,
    hc,
    weights,
    dsum,
    wx,
    wy,
    yb,
    ex,
    ey,
    gx,
    gy,
    gc,
    piece,
    pieces,
    slots,
    owned,
    load_sem,
    ks_send,
    ks_recv,
    z_send,
    z_recv,
    one_send,
    one_recv,
    two_send,
    two_recv,
    local_sem,
):
    f32, bf16 = jnp.float32, jnp.bfloat16
    ax = lax.axis_index("gx")
    ay = lax.axis_index("gy")
    parity = lax.rem(ax, 2)
    parity_f = parity.astype(f32)

    def device(dx, dy):
        return (lax.rem(ax + dx + ROWS, ROWS), lax.rem(ay + dy + COLS, COLS))

    small = [
        pltpu.make_async_copy(ids_hbm, ids, load_sem.at[4]),
        pltpu.make_async_copy(phase_hbm, phase, load_sem.at[5]),
        pltpu.make_async_copy(owner_hbm, owner, load_sem.at[6]),
    ]
    loads = [
        pltpu.make_async_copy(
            basis.at[pl.ds(1024 * g, 1024)], raw.at[pl.ds(1024 * g, 1024)], load_sem.at[g]
        )
        for g in range(4)
    ]
    for copy in small + loads:
        copy.start()

    barrier = pltpu.get_barrier_semaphore()

    def greet(off, carry):
        pl.semaphore_signal(
            barrier, inc=1, device_id=(ax, lax.rem(ay + off, COLS)), device_id_type=MESH
        )
        return carry

    for dx, dy in REGIONS:
        if dx != 0:
            pl.semaphore_signal(barrier, inc=1, device_id=device(dx, dy), device_id_type=MESH)
    lax.fori_loop(1, COLS, greet, 0)

    kp[...] = jnp.zeros_like(kp)
    frame_own[...] = jnp.zeros_like(frame_own)
    frame_x[...] = jnp.zeros_like(frame_x)
    frame_y[...] = jnp.zeros_like(frame_y)
    zero = jnp.zeros((8, K, NZ), f32)
    for edge in (0, CX + 1):
        zf[edge] = zero
        zs[edge] = zero
    zmy[0] = zero[0]
    zmy[CX + 1] = zero[0]
    yb[0] = jnp.zeros((CY, 2 * K, NZ), bf16)

    for copy in small:
        copy.wait()
    table = phase[...].astype(f32)
    for x in range(CX):
        cell = ids[x]
        value = jnp.zeros((CY, NZ), f32)
        for p in range(8):
            value = jnp.where(cell == p, table[0:1, p : p + 1], value)
        kp[x + 1, 8:16, :] = value
    for side, y in ((0, 0), (1, CY - 1)):
        for x in range(CX):
            kface[side, x : x + 1, :] = kp[x + 1, 8 + y : 9 + y, :]

    for g in range(4):
        loads[g].wait()

        def widen(i, carry, g=g):
            at = pl.multiple_of(1024 * g + i * 128, 128)
            to = pl.multiple_of(PITCH * 8 * g + i * PITCH, 8)
            stage[pl.ds(to, 128), :] = raw[pl.ds(at, 128), :].astype(f32)
            return carry

        lax.fori_loop(0, 8, widen, 0)

    def turn(x, carry):
        for y in range(CY):
            r = x * CY + y
            slab = jnp.concatenate(
                [stage[pl.ds(8 * PITCH * g + r, 8, stride=PITCH), :] for g in range(4)], axis=0
            )
            zf[x + 1, y] = slab
            zs[x + 1, y] = pltpu.roll(slab, NZ - 1, 1)
            zb[x, y] = slab.astype(bf16)
        return carry

    lax.fori_loop(0, CX, turn, 0)

    pl.semaphore_wait(barrier, COLS - 1 + 6)

    sends = []
    for i, (dx, dy) in enumerate(REGIONS):
        other = REGIONS.index((-dx, -dy))
        if dx == 0:
            src, dst = kface.at[0 if dy < 0 else 1], ky.at[0 if dy > 0 else 1]
        else:
            src, dst = kp.at[1 if dx < 0 else CX, pl.ds(8, 8), :], kx.at[other]
        sends.append(
            pltpu.make_async_remote_copy(
                src_ref=src,
                dst_ref=dst,
                send_sem=ks_send.at[i],
                recv_sem=ks_recv.at[other],
                device_id=device(dx, dy),
                device_id_type=MESH,
            )
        )
    moves = [
        pltpu.make_async_remote_copy(
            src_ref=zb.at[:, 7 - 7 * parity],
            dst_ref=hy,
            send_sem=z_send.at[0],
            recv_sem=z_recv.at[0],
            device_id=(ax, lax.rem(ay + 1 - 2 * parity + COLS, COLS)),
            device_id_type=MESH,
        )
    ]
    for side, dx in ((0, -1), (1, 1)):
        moves.append(
            pltpu.make_async_remote_copy(
                src_ref=zb.at[0 if dx < 0 else CX - 1],
                dst_ref=hx.at[1 - side],
                send_sem=z_send.at[1 + side],
                recv_sem=z_recv.at[2 - side],
                device_id=device(dx, 0),
                device_id_type=MESH,
            )
        )
    for c, (dx, dy) in enumerate(CORNERS):
        moves.append(
            pltpu.make_async_remote_copy(
                src_ref=zb.at[0 if dx < 0 else CX - 1, 0 if dy < 0 else CY - 1],
                dst_ref=hc.at[3 - c],
                send_sem=z_send.at[3 + c],
                recv_sem=z_recv.at[6 - c],
                device_id=device(dx, dy),
                device_id_type=MESH,
            )
        )
    for copy in sends + moves:
        copy.start()

    def harmonic(own, near, o):
        coef = 2.0 / (9.0 * (o[0] * o[0] + o[1] * o[1] + o[2] * o[2]))
        return (coef * own) * near / jnp.maximum(own + near, 0.05)

    def below(value):
        lane = lax.broadcasted_iota(jnp.int32, value.shape, 1)
        return jnp.where(lane == 0, 0.0, pltpu.roll(value, 1, 1))

    def above(value):
        lane = lax.broadcasted_iota(jnp.int32, value.shape, 1)
        return jnp.where(lane == NZ - 1, 0.0, pltpu.roll(value, NZ - 1, 1))

    for x in range(CX + 2):
        row = kp[x]
        kz[0, x] = below(row)
        kz[1, x] = row
        kz[2, x] = above(row)

    def weigh(x, carry):
        own = kp[x + 1, 8:16, :]
        total = REACT * own
        for o in OFFSETS:
            near = kz[o[2] + 1, x + 1 + o[0], 8 + o[1] : 16 + o[1], :]
            weight = harmonic(own, near, o)
            if o in HALF:
                weights[HALF.index(o), x] = weight
            total = total + weight
        dsum[x] = 0.5 * total
        return carry

    lax.fori_loop(0, CX, weigh, 0)

    def contract(x, slot):
        left = jnp.concatenate([yb[slot, y] for y in range(CY)], axis=1)
        right = jnp.concatenate([zb[x, y] for y in range(CY)], axis=1)
        return lax.dot_general(left, right, LAST, preferred_element_type=f32)

    def interior(x, acc):
        acc = acc + contract(jnp.maximum(x - 1, 0), x)
        for y in range(CY):
            value = dsum[x, y : y + 1, :] * zf[x + 1, y]
            for i, (ox, oy, oz) in enumerate(HALF):
                if not 0 <= y + oy < CY:
                    continue
                field = zf if oz == 0 else zs
                w = weights[i, x, y : y + 1, :]
                value = value - w * field[x + 1 + ox, y + oy]
            high, low = split(value)
            yb[x + 1, y, 0:K, :] = high
            yb[x + 1, y, K : 2 * K, :] = low
        return acc

    acc = lax.fori_loop(0, CX, interior, jnp.zeros((2 * K, K), f32))
    acc = acc + contract(CX - 1, CX)

    for copy in sends:
        copy.wait()
    low_x = (ax > 0).astype(f32)
    high_x = (ax < ROWS - 1).astype(f32)
    low_y = (ay > 0).astype(f32)
    high_y = (ay < COLS - 1).astype(f32)
    for side, dx, keep in ((0, -1, low_x), (1, 1, high_x)):
        near = kx[REGIONS.index((dx, 0))] * keep
        frame_x[1, side, 8:16, :] = near
    for side, dy, keep in ((0, -1, low_y), (1, 1, high_y)):
        y = 7 if dy < 0 else 0
        frame_y[1, side, 8:24, :] = ky[side] * keep
        for at, dx, keep_x in ((7, -1, low_x), (24, 1, high_x)):
            corner = kx[REGIONS.index((dx, dy)), y : y + 1, :]
            frame_y[1, side, at : at + 1, :] = corner * (keep * keep_x)
        frame_own[1, side, 8:24, :] = kface[side]
    for frame in (frame_x, frame_y, frame_own):
        for side in range(2):
            row = frame[1, side]
            frame[0, side] = below(row)
            frame[2, side] = above(row)

    NINE = [(i, j) for i in (-1, 0, 1) for j in (-1, 0, 1)]
    for side, dx in ((0, -1), (1, 1)):
        x = 0 if dx < 0 else CX - 1
        own = kp[x + 1, 8:16, :]
        total = jnp.zeros_like(own)
        for oy, oz in NINE:
            near = frame_x[oz + 1, side, 8 + oy : 16 + oy, :]
            total = total + harmonic(own, near, (dx, oy, oz))
        for y in range(CY):
            high, low = split(total[y : y + 1] * zf[x + 1, y])
            ex[side, y, 0:K, :] = high
            ex[side, y, K : 2 * K, :] = low
    for side, dy in ((0, -1), (1, 1)):
        own = kface[side]
        total = jnp.zeros_like(own)
        for ox, oz in NINE:
            near = frame_y[oz + 1, side, 8 + ox : 24 + ox, :]
            total = total + harmonic(own, near, (ox, dy, oz))
        for x in range(CX):
            high, low = split(total[x : x + 1] * zf[x + 1, 0 if dy < 0 else CY - 1])
            ey[side, x, 0:K, :] = high
            ey[side, x, K : 2 * K, :] = low
    outer = jnp.zeros((2 * K, K), f32)
    for side in range(2):
        x = 0 if side == 0 else CX - 1
        y = 0 if side == 0 else CY - 1
        outer = outer + lax.dot_general(
            jnp.concatenate([ex[side, i] for i in range(CY)], axis=1),
            jnp.concatenate([zb[x, i] for i in range(CY)], axis=1),
            LAST,
            preferred_element_type=f32,
        )
        outer = outer + lax.dot_general(
            jnp.concatenate([ey[side, i] for i in range(CX)], axis=1),
            jnp.concatenate([zb[i, y] for i in range(CX)], axis=1),
            LAST,
            preferred_element_type=f32,
        )
    half = acc[:K] + acc[K:]
    diagonal = (half + half.T + outer[:K] + outer[K:]) * (1.0 / (CX * CY * NZ))

    for side, dx in ((0, -1), (1, 1)):
        x = 0 if dx < 0 else CX - 1
        for y in range(CY):
            zmx[side, y] = pltpu.roll(zf[x + 1, y], 1, 1)
        own = frame_x[1, side, 8:16, :]
        for i, (oy, oz) in enumerate(NINE):
            near = kz[oz + 1, x + 1, 8 + oy : 16 + oy, :]
            wx[side, i] = harmonic(own, near, (dx, oy, oz))
        for y in range(CY):
            value = jnp.zeros((K, NZ), f32)
            for i, (oy, oz) in enumerate(NINE):
                if not 0 <= y + oy < CY:
                    continue
                field = (zmx[side, y + oy], zf[x + 1, y + oy], zs[x + 1, y + oy])[oz + 1]
                value = value - wx[side, i, y : y + 1, :] * field
            high, low = split(value)
            gx[side, y, 0:K, :] = high
            gx[side, y, K : 2 * K, :] = low
    for c, (dx, dy) in enumerate(CORNERS):
        x = 0 if dx < 0 else CX - 1
        y = 0 if dy < 0 else CY - 1
        side = 0 if dx < 0 else 1
        at = 7 if dx < 0 else 24
        own = frame_y[1, 0 if dy < 0 else 1, at : at + 1, :]
        value = jnp.zeros((K, NZ), f32)
        for oz in (-1, 0, 1):
            near = kz[oz + 1, x + 1, 8 + y : 9 + y, :]
            field = (zmx[side, y], zf[x + 1, y], zs[x + 1, y])[oz + 1]
            value = value - harmonic(own, near, (dx, dy, oz)) * field
        high, low = split(value)
        gc[c, 0:K, :] = high
        gc[c, K : 2 * K, :] = low
    y_edge = 7 * parity
    own = frame_y[1, parity, 8:24, :]
    for i, (ox, oz) in enumerate(NINE):
        near = frame_own[oz + 1, parity, 8 + ox : 24 + ox, :]
        wy[i] = harmonic(own, near, (ox, 1, oz))

    def lower(x, carry):
        zmy[x + 1] = pltpu.roll(zf[x + 1, y_edge], 1, 1)
        return carry

    lax.fori_loop(0, CX, lower, 0, unroll=4)

    def face(x, carry):
        value = jnp.zeros((K, NZ), f32)
        for i, (ox, oz) in enumerate(NINE):
            at = x + 1 + ox
            field = (zmy[at], zf[at, y_edge], zs[at, y_edge])[oz + 1]
            value = value - wy[i, pl.ds(x, 1), :] * field
        high, low = split(value)
        gy[x, 0:K, :] = high
        gy[x, K : 2 * K, :] = low
        return carry

    lax.fori_loop(0, CX, face, 0, unroll=4)

    width = COLS
    own_row = jnp.broadcast_to(owner[...], (width, width))
    i_sub = lax.broadcasted_iota(jnp.int32, (width, width), 0)
    i_lane = lax.broadcasted_iota(jnp.int32, (width, width), 1)
    own_f = own_row.astype(f32)
    own_col = jnp.sum(jnp.where(i_sub == i_lane, own_f, 0.0), axis=1, keepdims=True)
    before = (own_col == own_f) & (i_sub < i_lane)
    rank = jnp.sum(jnp.where(before, 1.0, 0.0), axis=0, keepdims=True)
    code = jnp.broadcast_to(own_f[0:1] * 4.0 + rank, (8, width)).astype(bf16)
    e_sub = lax.broadcasted_iota(jnp.int32, (width, NZ), 0)
    e_lane = lax.broadcasted_iota(jnp.int32, (width, NZ), 1)
    step = 2 * parity - 1
    e_from = e_lane // 4 + jnp.where(e_lane % 4 == 3, step, 0)
    expand = jnp.where(e_from == e_sub, 1.0, 0.0).astype(bf16)
    wide = jnp.dot(code, expand, preferred_element_type=f32)[0:1].astype(jnp.int32)
    wide_owner = wide // 4
    wide_rank = wide - wide_owner * 4
    lane1 = lax.broadcasted_iota(jnp.int32, (1, NZ), 1)
    part = lane1 % 4
    target = wide_owner * 8 + wide_rank * 2 + jnp.where(part == 3, 1 - parity, part)
    target = jnp.where(part == 2, wide_owner * 8 + 6, target)
    end = (lane1 // 4 + step < 0) | (lane1 // 4 + step >= width)
    target = jnp.where((part == 3) & end, -1, target)
    p_sub = lax.broadcasted_iota(jnp.int32, (COLS * 8, NZ), 0)
    route = jnp.where(p_sub == target, 1.0, 0.0).astype(bf16)
    my_rank = jnp.sum(
        jnp.where(lax.broadcasted_iota(jnp.int32, (1, width), 1) == ay, rank, 0.0),
        axis=1,
        keepdims=True,
    )
    quarter = (lax.broadcasted_iota(jnp.int32, (K, NZ), 1) // K).astype(f32)

    for copy in moves:
        copy.wait()

    def meet(left, right):
        product = lax.dot_general(left, right, LAST, preferred_element_type=f32)
        return product[:K] + product[K:]

    blocks = {}
    for side, dx in ((0, -1), (1, 1)):
        blocks[(dx, 0)] = meet(
            jnp.concatenate([gx[side, y] for y in range(CY)], axis=1),
            jnp.concatenate([hx[side, y] for y in range(CY)], axis=1),
        )
    for c, region in enumerate(CORNERS):
        blocks[region] = meet(gc[c], hc[c])
    across = meet(
        jnp.concatenate([gy[x] for x in range(CX)], axis=1),
        jnp.concatenate([hy[x] for x in range(CX)], axis=1),
    )
    back = across.T
    none = jnp.zeros_like(back)
    rows = [
        jnp.concatenate(
            [blocks[(-1, -1)], blocks[(-1, 0)], blocks[(-1, 1)], across * (1.0 - parity_f)],
            axis=1,
        ),
        jnp.concatenate(
            [across * parity_f, blocks[(1, -1)], blocks[(1, 0)], blocks[(1, 1)]], axis=1
        ),
        jnp.where(quarter == my_rank, jnp.concatenate([diagonal] * 4, axis=1), 0.0),
        jnp.concatenate([back * (1.0 - parity_f), none, none, back * parity_f], axis=1),
    ]
    flat = piece.reshape(4 * K, NZ)
    for l, value in enumerate(rows):
        flat[pl.ds(l, K, stride=4), :] = value

    def first(off, carry):
        to = lax.rem(ay + off, COLS)
        pltpu.make_async_remote_copy(
            src_ref=piece.at[to],
            dst_ref=pieces.at[ay],
            send_sem=one_send,
            recv_sem=one_recv,
            device_id=(ax, to),
            device_id_type=MESH,
        ).start()
        return carry

    lax.fori_loop(1, COLS, first, 0)
    keep = pltpu.make_async_copy(piece.at[ay], pieces.at[ay], local_sem.at[0])
    keep.start()
    keep.wait()
    many = pieces.at[pl.ds(0, COLS - 1)]
    pltpu.make_async_copy(many, many, one_recv).wait()

    got = pieces.reshape(4 * COLS, NZ)[...]
    a1 = got.astype(jnp.bfloat16)
    rest = got - a1.astype(f32)
    a2 = rest.astype(jnp.bfloat16)
    a3 = (rest - a2.astype(f32)).astype(jnp.bfloat16)
    slots[...] = (
        jnp.dot(route, a1, preferred_element_type=f32)
        + jnp.dot(route, a2, preferred_element_type=f32)
        + jnp.dot(route, a3, preferred_element_type=f32)
    ).reshape(COLS, 8, NZ)

    def second(off, carry):
        to = lax.rem(ay + off, COLS)
        pltpu.make_async_remote_copy(
            src_ref=slots.at[to],
            dst_ref=owned.at[ay],
            send_sem=two_send,
            recv_sem=two_recv,
            device_id=(ax, to),
            device_id_type=MESH,
        ).start()
        return carry

    lax.fori_loop(1, COLS, second, 0)
    keep = pltpu.make_async_copy(slots.at[ay], owned.at[ay], local_sem.at[1])
    keep.start()
    keep.wait()
    sent = piece.at[pl.ds(0, COLS - 1)]
    pltpu.make_async_copy(sent, sent, one_send).wait()
    many = owned.at[pl.ds(0, COLS - 1)]
    pltpu.make_async_copy(many, many, two_recv).wait()

    mine = owned.reshape(8 * COLS, NZ)
    for c in range(CAP):
        for half_row in range(2):
            value = mine[pl.ds(2 * c + half_row, K, stride=8), :]
            for q in range(4):
                out_coup[c, half_row * 4 + q] = value[:, q * K : (q + 1) * K]
    value = mine[pl.ds(6, K, stride=8), :]
    for c in range(CAP):
        out_diag[c] = value[:, c * K : (c + 1) * K]
    sent = slots.at[pl.ds(0, COLS - 1)]
    pltpu.make_async_copy(sent, sent, two_send).wait()


def shards(basis, phase_ids, phase_stiffness, owner_map):
    f32, bf16 = jnp.float32, jnp.bfloat16
    vmem = pltpu.VMEM
    dma = pltpu.SemaphoreType.DMA
    whole = pl.BlockSpec(memory_space=pltpu.VMEM)
    diag, coup = pl.pallas_call(
        kernel,
        out_shape=(
            jax.ShapeDtypeStruct((CAP, K, K), f32),
            jax.ShapeDtypeStruct((CAP, 8, K, K), f32),
        ),
        in_specs=[pl.BlockSpec(memory_space=pltpu.HBM)] * 4,
        out_specs=(whole, whole),
        scratch_shapes=[
            vmem((K * CX * CY, NZ), bf16),
            vmem((CX, CY, NZ), jnp.int32),
            vmem((1, 8), bf16),
            vmem((1, COLS), jnp.int32),
            vmem((K * PITCH, NZ), f32),
            vmem((CX + 2, CY, K, NZ), f32),
            vmem((CX + 2, CY, K, NZ), f32),
            vmem((CX, CY, K, NZ), bf16),
            vmem((2, CY, K, NZ), f32),
            vmem((CX + 2, K, NZ), f32),
            vmem((CX + 2, 24, NZ), f32),
            vmem((3, CX + 2, 24, NZ), f32),
            vmem((8, 8, NZ), f32),
            vmem((2, CX, NZ), f32),
            vmem((2, CX, NZ), f32),
            vmem((3, 2, 24, NZ), f32),
            vmem((3, 2, 32, NZ), f32),
            vmem((3, 2, 32, NZ), f32),
            vmem((2, CY, K, NZ), bf16),
            vmem((CX, K, NZ), bf16),
            vmem((4, K, NZ), bf16),
            vmem((13, CX, CY, NZ), f32),
            vmem((CX, CY, NZ), f32),
            vmem((2, 9, CY, NZ), f32),
            vmem((9, CX, NZ), f32),
            vmem((CX + 1, CY, 2 * K, NZ), bf16),
            vmem((2, CY, 2 * K, NZ), bf16),
            vmem((2, CX, 2 * K, NZ), bf16),
            vmem((2, CY, 2 * K, NZ), bf16),
            vmem((CX, 2 * K, NZ), bf16),
            vmem((4, 2 * K, NZ), bf16),
            vmem((K, 4, NZ), f32),
            vmem((COLS, 4, NZ), f32),
            vmem((COLS, 8, NZ), f32),
            vmem((COLS, 8, NZ), f32),
            dma((7,)),
            dma((8,)),
            dma((8,)),
            dma((7,)),
            dma((7,)),
            dma,
            dma,
            dma,
            dma,
            dma((2,)),
        ],
        compiler_params=pltpu.CompilerParams(
            collective_id=0, has_side_effects=True, vmem_limit_bytes=60 * 1024 * 1024
        ),
    )(
        basis.reshape(K * CX * CY, NZ),
        phase_ids,
        phase_stiffness.reshape(1, 8),
        owner_map,
    )
    return diag[None], coup[None]


def solution(mesh):
    return jax.shard_map(
        shards,
        mesh=mesh,
        in_specs=(P(None, "gx", "gy", None), P("gx", "gy", None), P(), P("gx", None)),
        out_specs=(P("gx", "gy", None, None), P("gx", "gy", None, None, None)),
        check_vma=False,
    )
```

time: 54.5 us -> 46.9 us (0.86); the launches traced: 53.5 us -> 46.4 us
  Pallas kernels: 48.7 us -> 42.6 us
  local copies, waits for them, and re-layouts: 4.09 us -> 3.19 us
    pallas_call x1, Pallas kernels: 48.7 us -> 42.6 us  [shards(): pl.pallas_call(kernel, out_shape=(jax.ShapeDtypeStruct((CAP, K, K), f32),...]
    unnamed x10 -> x2, local copies, waits for them, and re-layouts: 4.09 us -> 3.19 us
where the time goes in v2:
time: 46.9 us; the launch traced here: 46.4 us
  Pallas kernels  42.6 us (91%)
  local copies, waits for them, and re-layouts  3.19 us (7%)
  between operations  0.64 us (1%)
    pallas_call x1, Pallas kernels, shards(): pl.pallas_call(kernel, out_shape=(jax.ShapeDtypeStruct((CAP, K, K), f32),...  42.6 us
    unnamed x2, local copies, waits for them, and re-layouts  3.19 us

profile of v2, /device:TPU:24, one launch (start us, length us, event | category | flops | bytes accessed | tf_op | source)
XLA Modules:
  0.0 46.4 jit_solution(7260220708254395092)
XLA Ops:
  0.6 42.6 %shard_map.59 = (f32[3,32,32]{2,1,0:T(8,128)}, f32[3,8,32,32]{3,2,1,0:T(8,128)}) custom-call(bf16[4096,128]{1,0:T(8,128)(2,1)} %bitcast.4, s32[16,8,128]{2,1,0:T(8,128)} %ids_hbm.1, bf16[1,8]{1,0:T(2,128)(2,1)} %bitcast.7, s32[1,32]{1,0:T(1,128)} %owner_hbm.1), custom_call_target="tpu_custom_call" | custom-call | tf_op jit(solution)/shard_map/pallas_call | solution.py:539
  43.3 1.4 %copy.8 = f32[1,3,32,32]{3,2,1,0:T(8,128)} copy(f32[1,3,32,32]{3,2,1,0:T(8,128)} %bitcast.6) | data formatting | bytes 24576
  44.7 1.8 %copy.9 = f32[1,3,8,32,32]{4,3,2,1,0:T(8,128)} copy(f32[1,3,8,32,32]{4,3,2,1,0:T(8,128)} %bitcast.5) | data formatting | bytes 196608

commit v3 on v2

--- a/solution.py
+++ b/solution.py
@@ -23,6 +23,7 @@
 K, CX, CY, NZ = 32, 16, 8, 128
 ROWS, COLS = 16, 32
 PITCH = 136
+LEVELS = 32000.0
 LAST = (((1,), (1,)), ((), ()))
 
 
@@ -37,8 +38,7 @@
     ids_hbm,
     phase_hbm,
     owner_hbm,
-    out_diag,
-    out_coup,
+    out,
     raw,
     ids,
     phase,
@@ -72,6 +72,7 @@
     gc,
     piece,
     pieces,
+    words,
     slots,
     owned,
     load_sem,
@@ -491,11 +492,25 @@
     rest = got - a1.astype(f32)
     a2 = rest.astype(jnp.bfloat16)
     a3 = (rest - a2.astype(f32)).astype(jnp.bfloat16)
-    slots[...] = (
+    value = (
         jnp.dot(route, a1, preferred_element_type=f32)
         + jnp.dot(route, a2, preferred_element_type=f32)
         + jnp.dot(route, a3, preferred_element_type=f32)
-    ).reshape(COLS, 8, NZ)
+    )
+    peak = jnp.max(jnp.abs(value), axis=1, keepdims=True)
+    power = jnp.ceil(jnp.log2(jnp.maximum(peak, 1e-30)))
+    coded = value * (jnp.exp2(-power) * LEVELS)
+    sub = lax.broadcasted_iota(jnp.int32, (COLS, 8, NZ), 1)
+    lane = lax.broadcasted_iota(jnp.int32, (COLS, 8, NZ), 2)
+    spread = jnp.broadcast_to(power, (COLS * 8, NZ)).reshape(COLS, 8, NZ)
+    powers = jnp.sum(jnp.where(sub == lane, spread, 0.0), axis=1, keepdims=True)
+    coded = jnp.where(sub == 7, powers, coded.reshape(COLS, 8, NZ))
+    words[...] = jnp.round(coded).astype(jnp.int32).reshape(COLS * 8, NZ)
+    packed = slots.reshape(4 * COLS, NZ)
+    for w in range(4):
+        low = words[pl.ds(w, COLS, stride=8), :]
+        high = words[pl.ds(w + 4, COLS, stride=8), :]
+        packed[pl.ds(w, COLS, stride=4), :] = (high << 16) | (low & 0xFFFF)
 
     def second(off, carry):
         to = lax.rem(ay + off, COLS)
@@ -518,17 +533,24 @@
     many = owned.at[pl.ds(0, COLS - 1)]
     pltpu.make_async_copy(many, many, two_recv).wait()
 
-    mine = owned.reshape(8 * COLS, NZ)
+    out[...] = owned[...]
+    sent = slots.at[pl.ds(0, COLS - 1)]
+    pltpu.make_async_copy(sent, sent, two_send).wait()
+
+
+def unpack(words, out_diag, out_coup):
+    f32 = jnp.float32
+    flat = words.reshape(4 * COLS, NZ)
+    got = [flat[pl.ds(w, K, stride=4), :] for w in range(4)]
+    rows = [(w << 16) >> 16 for w in got] + [w >> 16 for w in got]
+    rows = [row.astype(f32) for row in rows]
+    scale = jnp.exp2(rows[7]) * (1.0 / LEVELS)
+    rows = [row * scale[:, r : r + 1] for r, row in enumerate(rows[:7])]
     for c in range(CAP):
         for half_row in range(2):
-            value = mine[pl.ds(2 * c + half_row, K, stride=8), :]
             for q in range(4):
-                out_coup[c, half_row * 4 + q] = value[:, q * K : (q + 1) * K]
-    value = mine[pl.ds(6, K, stride=8), :]
-    for c in range(CAP):
-        out_diag[c] = value[:, c * K : (c + 1) * K]
-    sent = slots.at[pl.ds(0, COLS - 1)]
-    pltpu.make_async_copy(sent, sent, two_send).wait()
+                out_coup[c, half_row * 4 + q] = rows[2 * c + half_row][:, q * K : (q + 1) * K]
+        out_diag[c] = rows[6][:, c * K : (c + 1) * K]
 
 
 def shards(basis, phase_ids, phase_stiffness, owner_map):
@@ -536,14 +558,11 @@
     vmem = pltpu.VMEM
     dma = pltpu.SemaphoreType.DMA
     whole = pl.BlockSpec(memory_space=pltpu.VMEM)
-    diag, coup = pl.pallas_call(
+    packed = pl.pallas_call(
         kernel,
-        out_shape=(
-            jax.ShapeDtypeStruct((CAP, K, K), f32),
-            jax.ShapeDtypeStruct((CAP, 8, K, K), f32),
-        ),
+        out_shape=jax.ShapeDtypeStruct((COLS, 4, NZ), jnp.int32),
         in_specs=[pl.BlockSpec(memory_space=pltpu.HBM)] * 4,
-        out_specs=(whole, whole),
+        out_specs=whole,
         scratch_shapes=[
             vmem((K * CX * CY, NZ), bf16),
             vmem((CX, CY, NZ), jnp.int32),
@@ -578,8 +597,9 @@
             vmem((4, 2 * K, NZ), bf16),
             vmem((K, 4, NZ), f32),
             vmem((COLS, 4, NZ), f32),
-            vmem((COLS, 8, NZ), f32),
-            vmem((COLS, 8, NZ), f32),
+            vmem((COLS * 8, NZ), jnp.int32),
+            vmem((COLS, 4, NZ), jnp.int32),
+            vmem((COLS, 4, NZ), jnp.int32),
             dma((7,)),
             dma((8,)),
             dma((8,)),
@@ -600,6 +620,15 @@
         phase_stiffness.reshape(1, 8),
         owner_map,
     )
+    diag, coup = pl.pallas_call(
+        unpack,
+        out_shape=(
+            jax.ShapeDtypeStruct((CAP, K, K), f32),
+            jax.ShapeDtypeStruct((CAP, 8, K, K), f32),
+        ),
+        in_specs=[whole],
+        out_specs=(whole, whole),
+    )(packed)
     return diag[None], coup[None]
 
 

time: 46.9 us -> 44.3 us (0.945)
  local copies, waits for them, and re-layouts: 3.19 us -> 0 us
  Pallas kernels: 42.6 us -> 43.4 us
    unnamed x2 -> x0, local copies, waits for them, and re-layouts: 3.19 us -> none
    pallas_call x1 -> x2, Pallas kernels: 42.6 us -> 43.4 us  [the longest x1 41.6 us: shards(): pl.pallas_call(kernel, out_shape=jax.ShapeDtypeStruct((COLS, 4, NZ), jnp....]
where the time goes in v3:
time: 44.3 us; the launch traced here: 44.1 us
  Pallas kernels  43.4 us (98%)
  between operations  0.64 us (1%)
    pallas_call x1, Pallas kernels, shards(): pl.pallas_call(kernel, out_shape=jax.ShapeDtypeStruct((COLS, 4, NZ), jnp....  41.6 us
    pallas_call x1, Pallas kernels, shards(): pl.pallas_call(unpack, out_shape=(jax.ShapeDtypeStruct((CAP, K, K), f32),...  1.82 us

profile of v3, /device:TPU:24, one launch (start us, length us, event | category | flops | bytes accessed | tf_op | source)
XLA Modules:
  0.0 44.1 jit_solution(9682665632022246494)
XLA Ops:
  0.6 41.6 %shard_map.59.words = s32[32,4,128]{2,1,0:T(4,128)} custom-call(bf16[4096,128]{1,0:T(8,128)(2,1)} %bitcast.4, s32[16,8,128]{2,1,0:T(8,128)} %ids_hbm.1, bf16[1,8]{1,0:T(2,128)(2,1)} %bitcast.5, s32[1,32]{1,0:T(1,128)} %owner_hbm.1), custom_call_target="tpu_custom_call" | custom-call | tf_op jit(solution)/shard_map/pallas_call | solution.py:561
  42.3 1.8 %shard_map.60 = (f32[3,32,32]{2,1,0:T(8,128)}, f32[3,8,32,32]{3,2,1,0:T(8,128)}) custom-call(s32[32,4,128]{2,1,0:T(4,128)} %shard_map.59.words), custom_call_target="tpu_custom_call" | custom-call | tf_op jit(solution)/shard_map/pallas_call | solution.py:623

commit v4 on v3

--- a/solution.py
+++ b/solution.py
@@ -23,6 +23,8 @@
 K, CX, CY, NZ = 32, 16, 8, 128
 ROWS, COLS = 16, 32
 PITCH = 136
+FAR = sorted(range(1, COLS), key=lambda off: -min(off % 16, 16 - off % 16))
+BEFORE = 8
 LEVELS = 32000.0
 LAST = (((1,), (1,)), ((), ()))
 
@@ -111,16 +113,13 @@
 
     barrier = pltpu.get_barrier_semaphore()
 
-    def greet(off, carry):
+    for off in FAR:
         pl.semaphore_signal(
             barrier, inc=1, device_id=(ax, lax.rem(ay + off, COLS)), device_id_type=MESH
         )
-        return carry
-
     for dx, dy in REGIONS:
         if dx != 0:
             pl.semaphore_signal(barrier, inc=1, device_id=device(dx, dy), device_id_type=MESH)
-    lax.fori_loop(1, COLS, greet, 0)
 
     kp[...] = jnp.zeros_like(kp)
     frame_own[...] = jnp.zeros_like(frame_own)
@@ -169,7 +168,61 @@
             zb[x, y] = slab.astype(bf16)
         return carry
 
-    lax.fori_loop(0, CX, turn, 0)
+    lax.fori_loop(0, CX, turn, 0, unroll=4)
+
+    def harmonic(own, near, o):
+        coef = 2.0 / (9.0 * (o[0] * o[0] + o[1] * o[1] + o[2] * o[2]))
+        return (coef * own) * near / jnp.maximum(own + near, 0.05)
+
+    def below(value):
+        lane = lax.broadcasted_iota(jnp.int32, value.shape, 1)
+        return jnp.where(lane == 0, 0.0, pltpu.roll(value, 1, 1))
+
+    def above(value):
+        lane = lax.broadcasted_iota(jnp.int32, value.shape, 1)
+        return jnp.where(lane == NZ - 1, 0.0, pltpu.roll(value, NZ - 1, 1))
+
+    for x in range(CX + 2):
+        row = kp[x]
+        kz[0, x] = below(row)
+        kz[1, x] = row
+        kz[2, x] = above(row)
+
+    def weigh(x, carry):
+        own = kp[x + 1, 8:16, :]
+        total = REACT * own
+        for o in OFFSETS:
+            near = kz[o[2] + 1, x + 1 + o[0], 8 + o[1] : 16 + o[1], :]
+            weight = harmonic(own, near, o)
+            if o in HALF:
+                weights[HALF.index(o), x] = weight
+            total = total + weight
+        dsum[x] = 0.5 * total
+        return carry
+
+    lax.fori_loop(0, CX, weigh, 0, unroll=2)
+
+    def contract(x, slot):
+        left = jnp.concatenate([yb[slot, y] for y in range(CY)], axis=1)
+        right = jnp.concatenate([zb[x, y] for y in range(CY)], axis=1)
+        return lax.dot_general(left, right, LAST, preferred_element_type=f32)
+
+    def interior(x, acc):
+        acc = acc + contract(jnp.maximum(x - 1, 0), x)
+        for y in range(CY):
+            value = dsum[x, y : y + 1, :] * zf[x + 1, y]
+            for i, (ox, oy, oz) in enumerate(HALF):
+                if not 0 <= y + oy < CY:
+                    continue
+                field = zf if oz == 0 else zs
+                w = weights[i, x, y : y + 1, :]
+                value = value - w * field[x + 1 + ox, y + oy]
+            high, low = split(value)
+            yb[x + 1, y, 0:K, :] = high
+            yb[x + 1, y, K : 2 * K, :] = low
+        return acc
+
+    acc = lax.fori_loop(0, BEFORE, interior, jnp.zeros((2 * K, K), f32), unroll=4)
 
     pl.semaphore_wait(barrier, COLS - 1 + 6)
 
@@ -225,59 +278,7 @@
     for copy in sends + moves:
         copy.start()
 
-    def harmonic(own, near, o):
-        coef = 2.0 / (9.0 * (o[0] * o[0] + o[1] * o[1] + o[2] * o[2]))
-        return (coef * own) * near / jnp.maximum(own + near, 0.05)
-
-    def below(value):
-        lane = lax.broadcasted_iota(jnp.int32, value.shape, 1)
-        return jnp.where(lane == 0, 0.0, pltpu.roll(value, 1, 1))
-
-    def above(value):
-        lane = lax.broadcasted_iota(jnp.int32, value.shape, 1)
-        return jnp.where(lane == NZ - 1, 0.0, pltpu.roll(value, NZ - 1, 1))
-
-    for x in range(CX + 2):
-        row = kp[x]
-        kz[0, x] = below(row)
-        kz[1, x] = row
-        kz[2, x] = above(row)
-
-    def weigh(x, carry):
-        own = kp[x + 1, 8:16, :]
-        total = REACT * own
-        for o in OFFSETS:
-            near = kz[o[2] + 1, x + 1 + o[0], 8 + o[1] : 16 + o[1], :]
-            weight = harmonic(own, near, o)
-            if o in HALF:
-                weights[HALF.index(o), x] = weight
-            total = total + weight
-        dsum[x] = 0.5 * total
-        return carry
-
-    lax.fori_loop(0, CX, weigh, 0)
-
-    def contract(x, slot):
-        left = jnp.concatenate([yb[slot, y] for y in range(CY)], axis=1)
-        right = jnp.concatenate([zb[x, y] for y in range(CY)], axis=1)
-        return lax.dot_general(left, right, LAST, preferred_element_type=f32)
-
-    def interior(x, acc):
-        acc = acc + contract(jnp.maximum(x - 1, 0), x)
-        for y in range(CY):
-            value = dsum[x, y : y + 1, :] * zf[x + 1, y]
-            for i, (ox, oy, oz) in enumerate(HALF):
-                if not 0 <= y + oy < CY:
-                    continue
-                field = zf if oz == 0 else zs
-                w = weights[i, x, y : y + 1, :]
-                value = value - w * field[x + 1 + ox, y + oy]
-            high, low = split(value)
-            yb[x + 1, y, 0:K, :] = high
-            yb[x + 1, y, K : 2 * K, :] = low
-        return acc
-
-    acc = lax.fori_loop(0, CX, interior, jnp.zeros((2 * K, K), f32))
+    acc = lax.fori_loop(BEFORE, CX, interior, acc, unroll=4)
     acc = acc + contract(CX - 1, CX)
 
     for copy in sends:
@@ -468,7 +469,7 @@
     for l, value in enumerate(rows):
         flat[pl.ds(l, K, stride=4), :] = value
 
-    def first(off, carry):
+    for off in FAR:
         to = lax.rem(ay + off, COLS)
         pltpu.make_async_remote_copy(
             src_ref=piece.at[to],
@@ -478,9 +479,6 @@
             device_id=(ax, to),
             device_id_type=MESH,
         ).start()
-        return carry
-
-    lax.fori_loop(1, COLS, first, 0)
     keep = pltpu.make_async_copy(piece.at[ay], pieces.at[ay], local_sem.at[0])
     keep.start()
     keep.wait()
@@ -512,7 +510,7 @@
         high = words[pl.ds(w + 4, COLS, stride=8), :]
         packed[pl.ds(w, COLS, stride=4), :] = (high << 16) | (low & 0xFFFF)
 
-    def second(off, carry):
+    for off in FAR:
         to = lax.rem(ay + off, COLS)
         pltpu.make_async_remote_copy(
             src_ref=slots.at[to],
@@ -522,9 +520,6 @@
             device_id=(ax, to),
             device_id_type=MESH,
         ).start()
-        return carry
-
-    lax.fori_loop(1, COLS, second, 0)
     keep = pltpu.make_async_copy(slots.at[ay], owned.at[ay], local_sem.at[1])
     keep.start()
     keep.wait()

time: 44.3 us -> 42.5 us (0.959)
  the two profiles are of different devices: /device:TPU:24 before, /device:TPU:2 now
where the time goes in v4:
time: 42.5 us; the launch traced here: 42.3 us
  Pallas kernels  41.6 us (98%)
  between operations  0.64 us (2%)
    pallas_call x1, Pallas kernels, shards(): pl.pallas_call(kernel, out_shape=jax.ShapeDtypeStruct((COLS, 4, NZ), jnp....  39.8 us
    pallas_call x1, Pallas kernels, shards(): pl.pallas_call(unpack, out_shape=(jax.ShapeDtypeStruct((CAP, K, K), f32),...  1.82 us

profile of v4, /device:TPU:2, one launch (start us, length us, event | category | flops | bytes accessed | tf_op | source)
XLA Modules:
  0.0 42.3 jit_solution(4684056253363107345)
XLA Ops:
  0.6 39.8 %shard_map.59.words = s32[32,4,128]{2,1,0:T(4,128)} custom-call(bf16[4096,128]{1,0:T(8,128)(2,1)} %bitcast.4, s32[16,8,128]{2,1,0:T(8,128)} %ids_hbm.1, bf16[1,8]{1,0:T(2,128)(2,1)} %bitcast.5, s32[1,32]{1,0:T(1,128)} %owner_hbm.1), custom_call_target="tpu_custom_call" | custom-call | tf_op jit(solution)/shard_map/pallas_call | solution.py:556
  40.5 1.8 %shard_map.60 = (f32[3,32,32]{2,1,0:T(8,128)}, f32[3,8,32,32]{3,2,1,0:T(8,128)}) custom-call(s32[32,4,128]{2,1,0:T(4,128)} %shard_map.59.words), custom_call_target="tpu_custom_call" | custom-call | tf_op jit(solution)/shard_map/pallas_call | solution.py:618

commit v5 on v4

--- a/solution.py
+++ b/solution.py
@@ -25,7 +25,10 @@
 PITCH = 136
 FAR = sorted(range(1, COLS), key=lambda off: -min(off % 16, 16 - off % 16))
 BEFORE = 8
-LEVELS = 32000.0
+RING = COLS // 2
+NEAR = sorted(
+    [(d, f) for d in range(8) for f in range(2) if (d, f) != (3, 0)], key=lambda t: -abs(t[0] - 3)
+)
 LAST = (((1,), (1,)), ((), ()))
 
 
@@ -74,7 +77,6 @@
     gc,
     piece,
     pieces,
-    words,
     slots,
     owned,
     load_sem,
@@ -410,21 +412,23 @@
     before = (own_col == own_f) & (i_sub < i_lane)
     rank = jnp.sum(jnp.where(before, 1.0, 0.0), axis=0, keepdims=True)
     code = jnp.broadcast_to(own_f[0:1] * 4.0 + rank, (8, width)).astype(bf16)
-    e_sub = lax.broadcasted_iota(jnp.int32, (width, NZ), 0)
-    e_lane = lax.broadcasted_iota(jnp.int32, (width, NZ), 1)
+    wide_n = 8 * width
+    e_sub = lax.broadcasted_iota(jnp.int32, (width, wide_n), 0)
+    e_lane = lax.broadcasted_iota(jnp.int32, (width, wide_n), 1)
     step = 2 * parity - 1
-    e_from = e_lane // 4 + jnp.where(e_lane % 4 == 3, step, 0)
+    e_from = e_lane // 8 + jnp.where(e_lane % 4 == 3, step, 0)
     expand = jnp.where(e_from == e_sub, 1.0, 0.0).astype(bf16)
     wide = jnp.dot(code, expand, preferred_element_type=f32)[0:1].astype(jnp.int32)
     wide_owner = wide // 4
     wide_rank = wide - wide_owner * 4
-    lane1 = lax.broadcasted_iota(jnp.int32, (1, NZ), 1)
+    lane1 = lax.broadcasted_iota(jnp.int32, (1, wide_n), 1)
     part = lane1 % 4
-    target = wide_owner * 8 + wide_rank * 2 + jnp.where(part == 3, 1 - parity, part)
-    target = jnp.where(part == 2, wide_owner * 8 + 6, target)
-    end = (lane1 // 4 + step < 0) | (lane1 // 4 + step >= width)
-    target = jnp.where((part == 3) & end, -1, target)
-    p_sub = lax.broadcasted_iota(jnp.int32, (COLS * 8, NZ), 0)
+    row = jnp.where(part == 2, 6, wide_rank * 2 + jnp.where(part == 3, 1 - parity, part))
+    place = (wide_owner % RING - ay % RING + RING + 3) % RING
+    target = place * 32 + (wide_owner // RING) * 16 + ((lane1 // 4) % 2) * 8 + row
+    end = (lane1 // 8 + step < 0) | (lane1 // 8 + step >= width)
+    target = jnp.where((place >= 8) | ((part == 3) & end), -1, target)
+    p_sub = lax.broadcasted_iota(jnp.int32, (16 * 16, wide_n), 0)
     route = jnp.where(p_sub == target, 1.0, 0.0).astype(bf16)
     my_rank = jnp.sum(
         jnp.where(lax.broadcasted_iota(jnp.int32, (1, width), 1) == ay, rank, 0.0),
@@ -465,87 +469,73 @@
         jnp.where(quarter == my_rank, jnp.concatenate([diagonal] * 4, axis=1), 0.0),
         jnp.concatenate([back * (1.0 - parity_f), none, none, back * parity_f], axis=1),
     ]
-    flat = piece.reshape(4 * K, NZ)
     for l, value in enumerate(rows):
-        flat[pl.ds(l, K, stride=4), :] = value
+        piece.reshape(4 * K, NZ)[pl.ds(l, K, stride=4), :] = value
+
+    def pair(to):
+        return lax.rem(to, 8) * 2 + to // RING
 
     for off in FAR:
         to = lax.rem(ay + off, COLS)
         pltpu.make_async_remote_copy(
-            src_ref=piece.at[to],
+            src_ref=piece.at[pair(to)],
             dst_ref=pieces.at[ay],
             send_sem=one_send,
             recv_sem=one_recv,
             device_id=(ax, to),
             device_id_type=MESH,
         ).start()
-    keep = pltpu.make_async_copy(piece.at[ay], pieces.at[ay], local_sem.at[0])
+    keep = pltpu.make_async_copy(piece.at[pair(ay)], pieces.at[ay], local_sem.at[0])
     keep.start()
     keep.wait()
     many = pieces.at[pl.ds(0, COLS - 1)]
     pltpu.make_async_copy(many, many, one_recv).wait()
 
-    got = pieces.reshape(4 * COLS, NZ)[...]
-    a1 = got.astype(jnp.bfloat16)
+    got = pieces.reshape(8 * COLS, NZ)[...]
+    a1 = got.astype(bf16)
     rest = got - a1.astype(f32)
-    a2 = rest.astype(jnp.bfloat16)
-    a3 = (rest - a2.astype(f32)).astype(jnp.bfloat16)
-    value = (
+    a2 = rest.astype(bf16)
+    a3 = (rest - a2.astype(f32)).astype(bf16)
+    slots[...] = (
         jnp.dot(route, a1, preferred_element_type=f32)
         + jnp.dot(route, a2, preferred_element_type=f32)
         + jnp.dot(route, a3, preferred_element_type=f32)
-    )
-    peak = jnp.max(jnp.abs(value), axis=1, keepdims=True)
-    power = jnp.ceil(jnp.log2(jnp.maximum(peak, 1e-30)))
-    coded = value * (jnp.exp2(-power) * LEVELS)
-    sub = lax.broadcasted_iota(jnp.int32, (COLS, 8, NZ), 1)
-    lane = lax.broadcasted_iota(jnp.int32, (COLS, 8, NZ), 2)
-    spread = jnp.broadcast_to(power, (COLS * 8, NZ)).reshape(COLS, 8, NZ)
-    powers = jnp.sum(jnp.where(sub == lane, spread, 0.0), axis=1, keepdims=True)
-    coded = jnp.where(sub == 7, powers, coded.reshape(COLS, 8, NZ))
-    words[...] = jnp.round(coded).astype(jnp.int32).reshape(COLS * 8, NZ)
-    packed = slots.reshape(4 * COLS, NZ)
-    for w in range(4):
-        low = words[pl.ds(w, COLS, stride=8), :]
-        high = words[pl.ds(w + 4, COLS, stride=8), :]
-        packed[pl.ds(w, COLS, stride=4), :] = (high << 16) | (low & 0xFFFF)
-
-    for off in FAR:
-        to = lax.rem(ay + off, COLS)
+    ).reshape(16, 16, NZ)
+
+    half_row = ay // RING
+    for d, f in NEAR:
+        x_half = lax.rem(half_row + f, 2)
+        to = x_half * RING + lax.rem(ay + d - 3 + RING, RING)
         pltpu.make_async_remote_copy(
-            src_ref=slots.at[to],
-            dst_ref=owned.at[ay],
+            src_ref=slots.at[2 * d + x_half],
+            dst_ref=owned.at[pair(ay)],
             send_sem=two_send,
             recv_sem=two_recv,
             device_id=(ax, to),
             device_id_type=MESH,
         ).start()
-    keep = pltpu.make_async_copy(slots.at[ay], owned.at[ay], local_sem.at[1])
+    keep = pltpu.make_async_copy(slots.at[6 + half_row], owned.at[pair(ay)], local_sem.at[1])
     keep.start()
     keep.wait()
-    sent = piece.at[pl.ds(0, COLS - 1)]
+    sent = pieces.at[pl.ds(0, COLS - 1)]
     pltpu.make_async_copy(sent, sent, one_send).wait()
-    many = owned.at[pl.ds(0, COLS - 1)]
+    many = owned.at[pl.ds(0, 15)]
     pltpu.make_async_copy(many, many, two_recv).wait()
-
     out[...] = owned[...]
-    sent = slots.at[pl.ds(0, COLS - 1)]
+    sent = slots.at[pl.ds(0, 15)]
     pltpu.make_async_copy(sent, sent, two_send).wait()
 
 
-def unpack(words, out_diag, out_coup):
-    f32 = jnp.float32
-    flat = words.reshape(4 * COLS, NZ)
-    got = [flat[pl.ds(w, K, stride=4), :] for w in range(4)]
-    rows = [(w << 16) >> 16 for w in got] + [w >> 16 for w in got]
-    rows = [row.astype(f32) for row in rows]
-    scale = jnp.exp2(rows[7]) * (1.0 / LEVELS)
-    rows = [row * scale[:, r : r + 1] for r, row in enumerate(rows[:7])]
+def deal(owned, out_diag, out_coup):
+    flat = owned.reshape(8 * K, NZ)
     for c in range(CAP):
         for half_row in range(2):
+            value = flat[pl.ds(2 * c + half_row, K, stride=8), :]
             for q in range(4):
-                out_coup[c, half_row * 4 + q] = rows[2 * c + half_row][:, q * K : (q + 1) * K]
-        out_diag[c] = rows[6][:, c * K : (c + 1) * K]
+                out_coup[c, half_row * 4 + q] = value[:, q * K : (q + 1) * K]
+    value = flat[pl.ds(6, K, stride=8), :]
+    for c in range(CAP):
+        out_diag[c] = value[:, c * K : (c + 1) * K]
 
 
 def shards(basis, phase_ids, phase_stiffness, owner_map):
@@ -553,9 +543,9 @@
     vmem = pltpu.VMEM
     dma = pltpu.SemaphoreType.DMA
     whole = pl.BlockSpec(memory_space=pltpu.VMEM)
-    packed = pl.pallas_call(
+    owned = pl.pallas_call(
         kernel,
-        out_shape=jax.ShapeDtypeStruct((COLS, 4, NZ), jnp.int32),
+        out_shape=jax.ShapeDtypeStruct((16, 16, NZ), f32),
         in_specs=[pl.BlockSpec(memory_space=pltpu.HBM)] * 4,
         out_specs=whole,
         scratch_shapes=[
@@ -590,11 +580,10 @@
             vmem((2, CY, 2 * K, NZ), bf16),
             vmem((CX, 2 * K, NZ), bf16),
             vmem((4, 2 * K, NZ), bf16),
-            vmem((K, 4, NZ), f32),
-            vmem((COLS, 4, NZ), f32),
-            vmem((COLS * 8, NZ), jnp.int32),
-            vmem((COLS, 4, NZ), jnp.int32),
-            vmem((COLS, 4, NZ), jnp.int32),
+            vmem((16, 8, NZ), f32),
+            vmem((COLS, 8, NZ), f32),
+            vmem((16, 16, NZ), f32),
+            vmem((16, 16, NZ), f32),
             dma((7,)),
             dma((8,)),
             dma((8,)),
@@ -616,14 +605,14 @@
         owner_map,
     )
     diag, coup = pl.pallas_call(
-        unpack,
+        deal,
         out_shape=(
             jax.ShapeDtypeStruct((CAP, K, K), f32),
             jax.ShapeDtypeStruct((CAP, 8, K, K), f32),
         ),
         in_specs=[whole],
         out_specs=(whole, whole),
-    )(packed)
+    )(owned)
     return diag[None], coup[None]
 
 

time: 42.5 us -> 42 us (0.988)
  the two profiles are of different devices: /device:TPU:2 before, /device:TPU:24 now
where the time goes in v5:
time: 42 us; the launch traced here: 41.8 us
  Pallas kernels  41.2 us (98%)
  between operations  0.64 us (2%)
    pallas_call x1, Pallas kernels, shards(): pl.pallas_call(kernel, out_shape=jax.ShapeDtypeStruct((16, 16, NZ), f32),...  39.4 us
    pallas_call x1, Pallas kernels, shards(): pl.pallas_call(deal, out_shape=(jax.ShapeDtypeStruct((CAP, K, K), f32), j...  1.8 us

profile of v5, /device:TPU:24, one launch (start us, length us, event | category | flops | bytes accessed | tf_op | source)
XLA Modules:
  0.0 41.8 jit_solution(3262471179437399135)
XLA Ops:
  0.6 39.4 %shard_map.59.owned = f32[16,16,128]{2,1,0:T(8,128)} custom-call(bf16[4096,128]{1,0:T(8,128)(2,1)} %bitcast.4, s32[16,8,128]{2,1,0:T(8,128)} %ids_hbm.1, bf16[1,8]{1,0:T(2,128)(2,1)} %bitcast.5, s32[1,32]{1,0:T(1,128)} %owner_hbm.1), custom_call_target="tpu_custom_call" | custom-call | tf_op jit(solution)/shard_map/pallas_call | solution.py:546
  40.0 1.8 %shard_map.60 = (f32[3,32,32]{2,1,0:T(8,128)}, f32[3,8,32,32]{3,2,1,0:T(8,128)}) custom-call(f32[16,16,128]{2,1,0:T(8,128)} %shard_map.59.owned), custom_call_target="tpu_custom_call" | custom-call | tf_op jit(solution)/shard_map/pallas_call | solution.py:607

commit v6 on v5

--- a/solution.py
+++ b/solution.py
@@ -24,7 +24,7 @@
 ROWS, COLS = 16, 32
 PITCH = 136
 FAR = sorted(range(1, COLS), key=lambda off: -min(off % 16, 16 - off % 16))
-BEFORE = 8
+BEFORE = 4
 RING = COLS // 2
 NEAR = sorted(
     [(d, f) for d in range(8) for f in range(2) if (d, f) != (3, 0)], key=lambda t: -abs(t[0] - 3)
@@ -75,6 +75,8 @@
     gx,
     gy,
     gc,
+    route,
+    mine,
     piece,
     pieces,
     slots,
@@ -224,6 +226,58 @@
             yb[x + 1, y, K : 2 * K, :] = low
         return acc
 
+    y_edge = 7 * parity
+
+    def lower(x, carry):
+        zmy[x + 1] = pltpu.roll(zf[x + 1, y_edge], 1, 1)
+        return carry
+
+    lax.fori_loop(0, CX, lower, 0, unroll=4)
+
+    for side in range(2):
+        for y in range(CY):
+            zmx[side, y] = pltpu.roll(zf[1 if side == 0 else CX, y], 1, 1)
+    for side in range(2):
+        frame_own[1, side, 8:24, :] = kface[side]
+        row = frame_own[1, side]
+        frame_own[0, side] = below(row)
+        frame_own[2, side] = above(row)
+
+    width = COLS
+    own_row = jnp.broadcast_to(owner[...], (width, width))
+    i_sub = lax.broadcasted_iota(jnp.int32, (width, width), 0)
+    i_lane = lax.broadcasted_iota(jnp.int32, (width, width), 1)
+    own_f = own_row.astype(f32)
+    own_col = jnp.sum(jnp.where(i_sub == i_lane, own_f, 0.0), axis=1, keepdims=True)
+    before = (own_col == own_f) & (i_sub < i_lane)
+    rank = jnp.sum(jnp.where(before, 1.0, 0.0), axis=0, keepdims=True)
+    code = jnp.broadcast_to(own_f[0:1] * 4.0 + rank, (8, width)).astype(bf16)
+    wide_n = 8 * width
+    e_sub = lax.broadcasted_iota(jnp.int32, (width, wide_n), 0)
+    e_lane = lax.broadcasted_iota(jnp.int32, (width, wide_n), 1)
+    step = 2 * parity - 1
+    e_from = e_lane // 8 + jnp.where(e_lane % 4 == 3, step, 0)
+    expand = jnp.where(e_from == e_sub, 1.0, 0.0).astype(bf16)
+    wide = jnp.dot(code, expand, preferred_element_type=f32)[0:1].astype(jnp.int32)
+    wide_owner = wide // 4
+    wide_rank = wide - wide_owner * 4
+    lane1 = lax.broadcasted_iota(jnp.int32, (1, wide_n), 1)
+    part = lane1 % 4
+    row = jnp.where(part == 2, 6, wide_rank * 2 + jnp.where(part == 3, 1 - parity, part))
+    place = (wide_owner % RING - ay % RING + RING + 3) % RING
+    target = place * 32 + (wide_owner // RING) * 16 + ((lane1 // 4) % 2) * 8 + row
+    end = (lane1 // 8 + step < 0) | (lane1 // 8 + step >= width)
+    target = jnp.where((place >= 8) | ((part == 3) & end), -1, target)
+    p_sub = lax.broadcasted_iota(jnp.int32, (16 * 16, wide_n), 0)
+    route[...] = jnp.where(p_sub == target, 1.0, 0.0).astype(bf16)
+    my_rank = jnp.sum(
+        jnp.where(lax.broadcasted_iota(jnp.int32, (1, width), 1) == ay, rank, 0.0),
+        axis=1,
+        keepdims=True,
+    )
+    quarter = (lax.broadcasted_iota(jnp.int32, (K, NZ), 1) // K).astype(f32)
+    mine[...] = jnp.where(quarter == my_rank, 1.0 / (CX * CY * NZ), 0.0)
+
     acc = lax.fori_loop(0, BEFORE, interior, jnp.zeros((2 * K, K), f32), unroll=4)
 
     pl.semaphore_wait(barrier, COLS - 1 + 6)
@@ -298,8 +352,7 @@
         for at, dx, keep_x in ((7, -1, low_x), (24, 1, high_x)):
             corner = kx[REGIONS.index((dx, dy)), y : y + 1, :]
             frame_y[1, side, at : at + 1, :] = corner * (keep * keep_x)
-        frame_own[1, side, 8:24, :] = kface[side]
-    for frame in (frame_x, frame_y, frame_own):
+    for frame in (frame_x, frame_y):
         for side in range(2):
             row = frame[1, side]
             frame[0, side] = below(row)
@@ -344,12 +397,13 @@
             preferred_element_type=f32,
         )
     half = acc[:K] + acc[K:]
-    diagonal = (half + half.T + outer[:K] + outer[K:]) * (1.0 / (CX * CY * NZ))
+    diagonal = half + half.T + outer[:K] + outer[K:]
+    piece.reshape(4 * K, NZ)[pl.ds(2, K, stride=4), :] = mine[...] * jnp.concatenate(
+        [diagonal] * 4, axis=1
+    )
 
     for side, dx in ((0, -1), (1, 1)):
         x = 0 if dx < 0 else CX - 1
-        for y in range(CY):
-            zmx[side, y] = pltpu.roll(zf[x + 1, y], 1, 1)
         own = frame_x[1, side, 8:16, :]
         for i, (oy, oz) in enumerate(NINE):
             near = kz[oz + 1, x + 1, 8 + oy : 16 + oy, :]
@@ -378,17 +432,10 @@
         high, low = split(value)
         gc[c, 0:K, :] = high
         gc[c, K : 2 * K, :] = low
-    y_edge = 7 * parity
     own = frame_y[1, parity, 8:24, :]
     for i, (ox, oz) in enumerate(NINE):
         near = frame_own[oz + 1, parity, 8 + ox : 24 + ox, :]
         wy[i] = harmonic(own, near, (ox, 1, oz))
-
-    def lower(x, carry):
-        zmy[x + 1] = pltpu.roll(zf[x + 1, y_edge], 1, 1)
-        return carry
-
-    lax.fori_loop(0, CX, lower, 0, unroll=4)
 
     def face(x, carry):
         value = jnp.zeros((K, NZ), f32)
@@ -401,41 +448,7 @@
         gy[x, K : 2 * K, :] = low
         return carry
 
-    lax.fori_loop(0, CX, face, 0, unroll=4)
-
-    width = COLS
-    own_row = jnp.broadcast_to(owner[...], (width, width))
-    i_sub = lax.broadcasted_iota(jnp.int32, (width, width), 0)
-    i_lane = lax.broadcasted_iota(jnp.int32, (width, width), 1)
-    own_f = own_row.astype(f32)
-    own_col = jnp.sum(jnp.where(i_sub == i_lane, own_f, 0.0), axis=1, keepdims=True)
-    before = (own_col == own_f) & (i_sub < i_lane)
-    rank = jnp.sum(jnp.where(before, 1.0, 0.0), axis=0, keepdims=True)
-    code = jnp.broadcast_to(own_f[0:1] * 4.0 + rank, (8, width)).astype(bf16)
-    wide_n = 8 * width
-    e_sub = lax.broadcasted_iota(jnp.int32, (width, wide_n), 0)
-    e_lane = lax.broadcasted_iota(jnp.int32, (width, wide_n), 1)
-    step = 2 * parity - 1
-    e_from = e_lane // 8 + jnp.where(e_lane % 4 == 3, step, 0)
-    expand = jnp.where(e_from == e_sub, 1.0, 0.0).astype(bf16)
-    wide = jnp.dot(code, expand, preferred_element_type=f32)[0:1].astype(jnp.int32)
-    wide_owner = wide // 4
-    wide_rank = wide - wide_owner * 4
-    lane1 = lax.broadcasted_iota(jnp.int32, (1, wide_n), 1)
-    part = lane1 % 4
-    row = jnp.where(part == 2, 6, wide_rank * 2 + jnp.where(part == 3, 1 - parity, part))
-    place = (wide_owner % RING - ay % RING + RING + 3) % RING
-    target = place * 32 + (wide_owner // RING) * 16 + ((lane1 // 4) % 2) * 8 + row
-    end = (lane1 // 8 + step < 0) | (lane1 // 8 + step >= width)
-    target = jnp.where((place >= 8) | ((part == 3) & end), -1, target)
-    p_sub = lax.broadcasted_iota(jnp.int32, (16 * 16, wide_n), 0)
-    route = jnp.where(p_sub == target, 1.0, 0.0).astype(bf16)
-    my_rank = jnp.sum(
-        jnp.where(lax.broadcasted_iota(jnp.int32, (1, width), 1) == ay, rank, 0.0),
-        axis=1,
-        keepdims=True,
-    )
-    quarter = (lax.broadcasted_iota(jnp.int32, (K, NZ), 1) // K).astype(f32)
+    lax.fori_loop(0, CX, face, 0, unroll=CX)
 
     for copy in moves:
         copy.wait()
@@ -466,10 +479,9 @@
         jnp.concatenate(
             [across * parity_f, blocks[(1, -1)], blocks[(1, 0)], blocks[(1, 1)]], axis=1
         ),
-        jnp.where(quarter == my_rank, jnp.concatenate([diagonal] * 4, axis=1), 0.0),
         jnp.concatenate([back * (1.0 - parity_f), none, none, back * parity_f], axis=1),
     ]
-    for l, value in enumerate(rows):
+    for l, value in zip((0, 1, 3), rows):
         piece.reshape(4 * K, NZ)[pl.ds(l, K, stride=4), :] = value
 
     def pair(to):
@@ -492,15 +504,11 @@
     pltpu.make_async_copy(many, many, one_recv).wait()
 
     got = pieces.reshape(8 * COLS, NZ)[...]
-    a1 = got.astype(bf16)
-    rest = got - a1.astype(f32)
-    a2 = rest.astype(bf16)
-    a3 = (rest - a2.astype(f32)).astype(bf16)
-    slots[...] = (
-        jnp.dot(route, a1, preferred_element_type=f32)
-        + jnp.dot(route, a2, preferred_element_type=f32)
-        + jnp.dot(route, a3, preferred_element_type=f32)
-    ).reshape(16, 16, NZ)
+    high, low = split(got)
+    both = jnp.dot(
+        route[...], jnp.concatenate([high, low], axis=1), preferred_element_type=f32
+    )
+    slots[...] = (both[:, :NZ] + both[:, NZ:]).reshape(16, 16, NZ)
 
     half_row = ay // RING
     for d, f in NEAR:
@@ -580,6 +588,8 @@
             vmem((2, CY, 2 * K, NZ), bf16),
             vmem((CX, 2 * K, NZ), bf16),
             vmem((4, 2 * K, NZ), bf16),
+            vmem((256, 256), bf16),
+            vmem((K, NZ), f32),
             vmem((16, 8, NZ), f32),
             vmem((COLS, 8, NZ), f32),
             vmem((16, 16, NZ), f32),

time: 42 us -> 42.3 us (level)
  no operation moved by 1% of the time
where the time goes in v6:
time: 42.3 us; the launch traced here: 41.9 us
  Pallas kernels  41.2 us (97%)
  between operations  0.64 us (2%)
    pallas_call x1, Pallas kernels, shards(): pl.pallas_call(kernel, out_shape=jax.ShapeDtypeStruct((16, 16, NZ), f32),...  39.4 us
    pallas_call x1, Pallas kernels, shards(): pl.pallas_call(deal, out_shape=(jax.ShapeDtypeStruct((CAP, K, K), f32), j...  1.8 us

profile of v6, /device:TPU:24, one launch (start us, length us, event | category | flops | bytes accessed | tf_op | source)
XLA Modules:
  0.0 41.9 jit_solution(4871092951641424904)
XLA Ops:
  0.6 39.4 %shard_map.59.owned = f32[16,16,128]{2,1,0:T(8,128)} custom-call(bf16[4096,128]{1,0:T(8,128)(2,1)} %bitcast.4, s32[16,8,128]{2,1,0:T(8,128)} %ids_hbm.1, bf16[1,8]{1,0:T(2,128)(2,1)} %bitcast.5, s32[1,32]{1,0:T(1,128)} %owner_hbm.1), custom_call_target="tpu_custom_call" | custom-call | tf_op jit(solution)/shard_map/pallas_call | solution.py:554
  40.1 1.8 %shard_map.60 = (f32[3,32,32]{2,1,0:T(8,128)}, f32[3,8,32,32]{3,2,1,0:T(8,128)}) custom-call(f32[16,16,128]{2,1,0:T(8,128)} %shard_map.59.owned), custom_call_target="tpu_custom_call" | custom-call | tf_op jit(solution)/shard_map/pallas_call | solution.py:617

commit v7 on v6

--- a/solution.py
+++ b/solution.py
@@ -331,14 +331,14 @@
                 device_id_type=MESH,
             )
         )
-    for copy in sends + moves:
+    for copy in sends + moves[3:] + moves[1:3] + moves[:1]:
         copy.start()
 
     acc = lax.fori_loop(BEFORE, CX, interior, acc, unroll=4)
     acc = acc + contract(CX - 1, CX)
 
     for copy in sends:
-        copy.wait()
+        copy.wait_recv()
     low_x = (ax > 0).astype(f32)
     high_x = (ax < ROWS - 1).astype(f32)
     low_y = (ay > 0).astype(f32)
@@ -451,7 +451,7 @@
     lax.fori_loop(0, CX, face, 0, unroll=CX)
 
     for copy in moves:
-        copy.wait()
+        copy.wait_recv()
 
     def meet(left, right):
         product = lax.dot_general(left, right, LAST, preferred_element_type=f32)
@@ -525,13 +525,17 @@
     keep = pltpu.make_async_copy(slots.at[6 + half_row], owned.at[pair(ay)], local_sem.at[1])
     keep.start()
     keep.wait()
+    for copy in sends + moves:
+        copy.wait_send()
     sent = pieces.at[pl.ds(0, COLS - 1)]
     pltpu.make_async_copy(sent, sent, one_send).wait()
     many = owned.at[pl.ds(0, 15)]
     pltpu.make_async_copy(many, many, two_recv).wait()
-    out[...] = owned[...]
+    keep = pltpu.make_async_copy(owned, out, local_sem.at[2])
+    keep.start()
     sent = slots.at[pl.ds(0, 15)]
     pltpu.make_async_copy(sent, sent, two_send).wait()
+    keep.wait()
 
 
 def deal(owned, out_diag, out_coup):
@@ -555,7 +559,7 @@
         kernel,
         out_shape=jax.ShapeDtypeStruct((16, 16, NZ), f32),
         in_specs=[pl.BlockSpec(memory_space=pltpu.HBM)] * 4,
-        out_specs=whole,
+        out_specs=pl.BlockSpec(memory_space=pltpu.HBM),
         scratch_shapes=[
             vmem((K * CX * CY, NZ), bf16),
             vmem((CX, CY, NZ), jnp.int32),
@@ -603,7 +607,7 @@
             dma,
             dma,
             dma,
-            dma((2,)),
+            dma((3,)),
         ],
         compiler_params=pltpu.CompilerParams(
             collective_id=0, has_side_effects=True, vmem_limit_bytes=60 * 1024 * 1024

time: 42.3 us -> 41.2 us (0.974)
  Pallas kernels: 41.2 us -> 40.4 us
    pallas_call x1, Pallas kernels: 39.4 us -> 38.6 us  [shards(): pl.pallas_call(kernel, out_shape=jax.ShapeDtypeStruct((16, 16, NZ), f32),...]
where the time goes in v7:
time: 41.2 us; the launch traced here: 41 us
  Pallas kernels  40.4 us (98%)
  between operations  0.64 us (2%)
    pallas_call x1, Pallas kernels, shards(): pl.pallas_call(kernel, out_shape=jax.ShapeDtypeStruct((16, 16, NZ), f32),...  38.6 us
    pallas_call x1, Pallas kernels, shards(): pl.pallas_call(deal, out_shape=(jax.ShapeDtypeStruct((CAP, K, K), f32), j...  1.8 us

profile of v7, /device:TPU:24, one launch (start us, length us, event | category | flops | bytes accessed | tf_op | source)
XLA Modules:
  0.0 41.0 jit_solution(1793271059743533147)
XLA Ops:
  0.6 38.6 %shard_map.59.owned = f32[16,16,128]{2,1,0:T(8,128)} custom-call(bf16[4096,128]{1,0:T(8,128)(2,1)} %bitcast.4, s32[16,8,128]{2,1,0:T(8,128)} %ids_hbm.1, bf16[1,8]{1,0:T(2,128)(2,1)} %bitcast.5, s32[1,32]{1,0:T(1,128)} %owner_hbm.1), custom_call_target="tpu_custom_call" | custom-call | tf_op jit(solution)/shard_map/pallas_call | solution.py:558
  39.2 1.8 %shard_map.60 = (f32[3,32,32]{2,1,0:T(8,128)}, f32[3,8,32,32]{3,2,1,0:T(8,128)}) custom-call(f32[16,16,128]{2,1,0:T(8,128)} %shard_map.59.owned), custom_call_target="tpu_custom_call" | custom-call | tf_op jit(solution)/shard_map/pallas_call | solution.py:621

commit v8 on v7

--- a/solution.py
+++ b/solution.py
@@ -331,7 +331,7 @@
                 device_id_type=MESH,
             )
         )
-    for copy in sends + moves[3:] + moves[1:3] + moves[:1]:
+    for copy in sends + moves[3:] + moves[:1] + moves[1:3]:
         copy.start()
 
     acc = lax.fori_loop(BEFORE, CX, interior, acc, unroll=4)

time: 41.2 us -> 41.2 us (level)
  no operation moved by 1% of the time
where the time goes in v8:
time: 41.2 us; the launch traced here: 41 us
  Pallas kernels  40.4 us (98%)
  between operations  0.64 us (2%)
    pallas_call x1, Pallas kernels, shards(): pl.pallas_call(kernel, out_shape=jax.ShapeDtypeStruct((16, 16, NZ), f32),...  38.6 us
    pallas_call x1, Pallas kernels, shards(): pl.pallas_call(deal, out_shape=(jax.ShapeDtypeStruct((CAP, K, K), f32), j...  1.8 us

profile of v8, /device:TPU:24, one launch (start us, length us, event | category | flops | bytes accessed | tf_op | source)
XLA Modules:
  0.0 41.0 jit_solution(12672485580956739493)
XLA Ops:
  0.6 38.6 %shard_map.59.owned = f32[16,16,128]{2,1,0:T(8,128)} custom-call(bf16[4096,128]{1,0:T(8,128)(2,1)} %bitcast.4, s32[16,8,128]{2,1,0:T(8,128)} %ids_hbm.1, bf16[1,8]{1,0:T(2,128)(2,1)} %bitcast.5, s32[1,32]{1,0:T(1,128)} %owner_hbm.1), custom_call_target="tpu_custom_call" | custom-call | tf_op jit(solution)/shard_map/pallas_call | solution.py:558
  39.2 1.8 %shard_map.60 = (f32[3,32,32]{2,1,0:T(8,128)}, f32[3,8,32,32]{3,2,1,0:T(8,128)}) custom-call(f32[16,16,128]{2,1,0:T(8,128)} %shard_map.59.owned), custom_call_target="tpu_custom_call" | custom-call | tf_op jit(solution)/shard_map/pallas_call | solution.py:621

commit v9 on v7

--- a/solution.py
+++ b/solution.py
@@ -24,7 +24,7 @@
 ROWS, COLS = 16, 32
 PITCH = 136
 FAR = sorted(range(1, COLS), key=lambda off: -min(off % 16, 16 - off % 16))
-BEFORE = 4
+BEFORE = 8
 RING = COLS // 2
 NEAR = sorted(
     [(d, f) for d in range(8) for f in range(2) if (d, f) != (3, 0)], key=lambda t: -abs(t[0] - 3)

time: 41.2 us -> 41.3 us (level)
  no operation moved by 1% of the time
where the time goes in v9:
time: 41.3 us; the launch traced here: 41.2 us
  Pallas kernels  40.5 us (98%)
  between operations  0.64 us (2%)
    pallas_call x1, Pallas kernels, shards(): pl.pallas_call(kernel, out_shape=jax.ShapeDtypeStruct((16, 16, NZ), f32),...  38.7 us
    pallas_call x1, Pallas kernels, shards(): pl.pallas_call(deal, out_shape=(jax.ShapeDtypeStruct((CAP, K, K), f32), j...  1.8 us

profile of v9, /device:TPU:24, one launch (start us, length us, event | category | flops | bytes accessed | tf_op | source)
XLA Modules:
  0.0 41.2 jit_solution(17137922459300382908)
XLA Ops:
  0.6 38.7 %shard_map.59.owned = f32[16,16,128]{2,1,0:T(8,128)} custom-call(bf16[4096,128]{1,0:T(8,128)(2,1)} %bitcast.4, s32[16,8,128]{2,1,0:T(8,128)} %ids_hbm.1, bf16[1,8]{1,0:T(2,128)(2,1)} %bitcast.5, s32[1,32]{1,0:T(1,128)} %owner_hbm.1), custom_call_target="tpu_custom_call" | custom-call | tf_op jit(solution)/shard_map/pallas_call | solution.py:558
  39.4 1.8 %shard_map.60 = (f32[3,32,32]{2,1,0:T(8,128)}, f32[3,8,32,32]{3,2,1,0:T(8,128)}) custom-call(f32[16,16,128]{2,1,0:T(8,128)} %shard_map.59.owned), custom_call_target="tpu_custom_call" | custom-call | tf_op jit(solution)/shard_map/pallas_call | solution.py:621
